TPU v7x, 128 devices: a whole 4x4x4 slice. The times are simulated.
128 devices in a mesh: col: 32 (over z, x, core), row: 4 (over y).
Axes of the slice: x: 4, y: 4, z: 4, core: 2. Of those that a mesh axis runs over, the one named last changes fastest.
Arguments:
- blocks: bfloat16 [16384, 128, 128], P(('col', 'row')), may hold values from -6 to 6
- dest: int32 [16384, 1], P(('col', 'row')), may hold values from 0 to 127; in each aligned block of 128 rows (0 to 127, 128 to 255, ...) at most 2 rows name the same one
- slot: int32 [16384], P(('col', 'row')), may hold values from 0 to 15
- template: bfloat16 [2048, 16384], P('row', 'col'), may hold values from -6 to 6
- kern_rows: bfloat16 [9, 31], replicated, may hold values from -1 to 1
- kern_cols: bfloat16 [9, 31], replicated, may hold values from -1 to 1
- coeffs: float32 [9, 3], replicated, may hold values from -3 to 3
Outputs:
- difference: bfloat16 [2048, 16384], P('row', 'col')
Inputs may be any that keep to these rules, and one draw needn't show every extreme that they name: `dest`: among the rows of one device, at most 2 blocks name one patch, a bound that some block reaches of them.
All inputs are finite; a program needn't handle non-finite values.
Results may differ from a plain program's by a relative error of at most 0.0049.
Values may be sent and summed in bfloat16 or wider, within the bound.
No kernel may reach another device: no remote copies, remote signals or barrier semaphores. Data moves between devices by JAX's collectives and lax.ppermute only.
A program may use at most 128 MiB of HBM per device.

v0:
```python
import functools

import jax
import jax.numpy as jnp
from jax import lax
from jax.experimental import pallas as pl
from jax.experimental.pallas import tpu as pltpu
from jax.sharding import PartitionSpec as P

HALF = 15
TAPS = 31
BASES = 9
GRID = 4
TB = 128
EXTENT = GRID * TB
AXES = ("col", "row")
STEP = 2048


def edge_shift(cells, axis, up):
    count = lax.axis_size(axis)
    if up:
        pairs = [(i, i + 1) for i in range(count - 1)]
    else:
        pairs = [(i + 1, i) for i in range(count - 1)]
    return lax.ppermute(cells, axis, pairs)


def with_halo(template):
    left = edge_shift(template[:, EXTENT - HALF:], "col", True)
    right = edge_shift(template[:, :HALF], "col", False)
    wide = jnp.concatenate([left, template, right], axis=1)
    above = edge_shift(wide[EXTENT - HALF:], "row", True)
    below = edge_shift(wide[:HALF], "row", False)
    tall = jnp.concatenate([above, wide, below], axis=0)
    return jnp.pad(tall, ((0, 2), (0, 98)))


def toeplitz(taps_row):
    spread = jnp.broadcast_to(taps_row, (TB, 2 * TB))
    return pltpu.roll(spread, 0, 1, stride=1, stride_axis=0).astype(jnp.bfloat16)


def model_kernel(coeffs_ref, origin_ref, padded_ref, rows_ref, cols_ref, model_ref, band_rows, band_cols, passed):
    for b in range(BASES):
        band_rows[b] = toeplitz(rows_ref[b:b + 1, :])
        band_cols[b] = toeplitz(cols_ref[b:b + 1, :])
    height_all = float(EXTENT * 4)
    width_all = float(EXTENT * 32)

    @pl.loop(0, GRID)
    def _(q):
        source = padded_ref[pl.ds(pl.multiple_of(q * TB, TB), 160), :]

        @pl.loop(0, BASES)
        def _(b):
            passed[b] = jnp.dot(
                band_rows[b][:, :160], source, preferred_element_type=jnp.float32
            ).astype(jnp.bfloat16)

        local_y = lax.broadcasted_iota(jnp.int32, (TB, TB), 0) + q * TB
        coord_y = 2.0 * (local_y.astype(jnp.float32) + (origin_ref[0] + 0.5)) / height_all - 1.0
        for p in range(GRID):
            local_x = lax.broadcasted_iota(jnp.int32, (TB, TB), 1) + p * TB
            coord_x = 2.0 * (local_x.astype(jnp.float32) + (origin_ref[1] + 0.5)) / width_all - 1.0
            total = jnp.zeros((TB, TB), jnp.float32)
            for b in range(BASES):
                image = lax.dot_general(
                    passed[b, :, p * TB:(p + 2) * TB],
                    band_cols[b],
                    (((1,), (1,)), ((), ())),
                    preferred_element_type=jnp.float32,
                )
                weight = coeffs_ref[3 * b] + coeffs_ref[3 * b + 1] * coord_x + coeffs_ref[3 * b + 2] * coord_y
                total = total + weight * image
            model_ref[pl.ds(pl.multiple_of(q * TB, TB), TB), p * TB:(p + 1) * TB] = total


def model_of(padded, kern_rows, kern_cols, coeffs):
    taps_rows = jnp.pad(kern_rows.astype(jnp.float32), ((0, 7), (0, 2 * TB - TAPS)))
    taps_cols = jnp.pad(kern_cols.astype(jnp.float32), ((0, 7), (0, 2 * TB - TAPS)))
    origin = jnp.stack([
        lax.axis_index("row").astype(jnp.float32) * EXTENT,
        lax.axis_index("col").astype(jnp.float32) * EXTENT,
    ])
    smem = pl.BlockSpec(memory_space=pltpu.SMEM)
    vmem = pl.BlockSpec(memory_space=pltpu.VMEM)
    return pl.pallas_call(
        model_kernel,
        out_shape=jax.ShapeDtypeStruct((EXTENT, EXTENT), jnp.float32),
        in_specs=[smem, smem, vmem, vmem, vmem],
        out_specs=vmem,
        scratch_shapes=[
            pltpu.VMEM((BASES, TB, 2 * TB), jnp.bfloat16),
            pltpu.VMEM((BASES, TB, 2 * TB), jnp.bfloat16),
            pltpu.VMEM((BASES, TB, 640), jnp.bfloat16),
        ],
        compiler_params=pltpu.CompilerParams(vmem_limit_bytes=24 << 20),
        cost_estimate=pl.CostEstimate(flops=3_000_000_000, bytes_accessed=2_000_000, transcendentals=0),
    )(coeffs.reshape(-1), origin, padded, taps_rows, taps_cols)


def merge_kernel(keys_ref, high_ref, rows_ref, out_ref, acc):
    step = pl.program_id(0)

    @pl.when(step == 0)
    def _():
        acc[...] = jnp.zeros_like(acc)

    upper = rows_ref[...] * high_ref[...]
    lower = rows_ref[...] - upper
    spread = jnp.concatenate([lower, upper], axis=1)
    keys = keys_ref[0]
    marks = lax.broadcasted_iota(jnp.int32, (256, STEP), 0).astype(jnp.bfloat16)
    for part in range(4):
        wanted = (keys - float(part * 256)).astype(jnp.bfloat16)
        chosen = jnp.where(marks == wanted, jnp.bfloat16(1), jnp.bfloat16(0))
        acc[part * 256:(part + 1) * 256, :] += jnp.dot(chosen, spread, preferred_element_type=jnp.float32)

    @pl.when(step == pl.num_programs(0) - 1)
    def _():
        whole = acc[...].reshape(TB, 8, 2 * TB)
        out_ref[...] = jnp.concatenate([whole[:, :, :TB], whole[:, :, TB:]], axis=1).astype(jnp.bfloat16)


def merged(keys, rows):
    count = keys.shape[0]
    steps = count // STEP
    places = ((keys // 16) * 8 + keys % 8).astype(jnp.float32).reshape(steps, 1, STEP)
    high = jnp.broadcast_to(((keys // 8) % 2).astype(jnp.bfloat16)[:, None], (count, TB))
    return pl.pallas_call(
        merge_kernel,
        grid=(steps,),
        out_shape=jax.ShapeDtypeStruct((TB, 16, TB), jnp.bfloat16),
        in_specs=[
            pl.BlockSpec((1, 1, STEP), lambda k: (k, 0, 0)),
            pl.BlockSpec((STEP, TB), lambda k: (k, 0)),
            pl.BlockSpec((STEP, TB), lambda k: (k, 0)),
        ],
        out_specs=pl.BlockSpec((TB, 16, TB), lambda k: (0, 0, 0)),
        scratch_shapes=[pltpu.VMEM((1024, 2 * TB), jnp.float32)],
        compiler_params=pltpu.CompilerParams(vmem_limit_bytes=24 << 20),
        cost_estimate=pl.CostEstimate(flops=8_600_000_000, bytes_accessed=9_000_000, transcendentals=0),
    )(places, high, rows)


def body(blocks, dest, slot, template, kern_rows, kern_cols, coeffs):
    keys = lax.all_gather(dest[:, 0] * 16 + slot, AXES, axis=0, tiled=True)
    rows = lax.all_to_all(blocks, AXES, split_axis=1, concat_axis=0, tiled=True).reshape(-1, TB)
    model = model_of(with_halo(template), kern_rows, kern_cols, coeffs)
    mine = lax.axis_index("col") * 4 + lax.axis_index("row")
    tiles = mine * 16 + jnp.arange(16, dtype=jnp.int32)
    counts = (keys[None, :] == tiles[:, None]).astype(jnp.float32).sum(axis=1)
    inverse = 1.0 / jnp.maximum(counts, 1.0)
    sums = merged(keys, rows)
    arrived = lax.all_to_all(sums, AXES, split_axis=0, concat_axis=0, tiled=True)
    science = (
        (arrived.astype(jnp.float32) * inverse[None, :, None])
        .reshape(TB, GRID, GRID, TB)
        .transpose(1, 0, 2, 3)
        .reshape(EXTENT, EXTENT)
    )
    return (science - model).astype(jnp.bfloat16)


def solution(mesh):
    placed = (P(AXES, None, None), P(AXES, None), P(AXES), P("row", "col"), P(), P(), P())
    return jax.shard_map(body, mesh=mesh, in_specs=placed, out_specs=P("row", "col"), check_vma=False)
```

profile of v0, /device:TPU:1, one launch (start us, length us, event | category | flops | bytes accessed | tf_op | source)
XLA Modules:
  0.0 153.2 jit_solution(4556639892292134059)
XLA Ops:
  0.0 6.9 %copy.17 = bf16[128,128,128]{2,0,1:T(8,128)(2,1)} copy(bf16[128,128,128]{2,1,0:T(8,128)(2,1)} %param.7) | data formatting | bytes 8388608 | tf_op args[0]
  6.9 0.0 copy-start
  6.9 0.0 copy-start.4
  6.9 0.0 copy-start.5
  6.9 0.0 copy-start.1
  6.9 0.0 copy-start.2
  6.9 0.0 copy-start.3
  6.9 12.0 %all-to-all-start = ((bf16[128,128,128]{2,0,1:T(8,128)(2,1)}), bf16[128,128,128]{2,0,1:T(8,128)(2,1)}, u32[]{:S(2)}, u32[]{:S(2)}) async-start(bf16[128,128,128]{2,0,1:T(8,128)(2,1)} %copy.17), calls=%async_computation | async-start | bytes 8388608 | tf_op jit(solution)/shard_map/all_to_all | solution.py:149
  18.9 0.0 copy-done
  18.9 0.1 fusion.25
  19.0 3.5 %collective-permute-start = (bf16[512,15]{1,0:T(8,128)(2,1)S(1)}, bf16[512,15]{1,0:T(8,128)(2,1)S(1)}, u32[]{:S(2)}, u32[]{:S(2)}) collective-permute-start(bf16[512,15]{1,0:T(8,128)(2,1)S(1)} %get-tuple-element.7), channel_id=1, source_target_pairs={{0,4},{4,8},{8,12},{12,16},{16,20},{20,24},{24,28},{28,32},{32,36}... | collective-permute-start | bytes 46088 | tf_op jit(solution)/shard_map/ppermute | solution.py:26
  22.5 1.9 %collective-permute-start.1 = (bf16[512,15]{1,0:T(8,128)(2,1)S(1)}, bf16[512,15]{1,0:T(8,128)(2,1)S(1)}, u32[]{:S(2)}, u32[]{:S(2)}) collective-permute-start(bf16[512,15]{1,0:T(8,128)(2,1)S(1)} %get-tuple-element.8), channel_id=1, source_target_pairs={{4,0},{8,4},{12,8},{16,12},{20,16},{24,20},{28,24},{32,28},{36,32}... | collective-permute-start | bytes 46088 | tf_op jit(solution)/shard_map/ppermute | solution.py:26
  24.5 0.0 copy-done.4
  24.5 0.0 copy-done.5
  24.5 81.1 %all-gather = s32[128,1,128]{2,1,0:T(1,128)S(1)} all-gather(s32[1,1,128]{2,1,0:T(1,128)S(1)} %fusion.24), channel_id=1, replica_groups=mesh['col'=32,'row'=4] {'col','row'}, dimensions={0}, use_global_device_ids=true | all-gather | bytes 66048 | tf_op jit(solution)/shard_map/all_gather | solution.py:148
  105.6 0.0 copy-done.1
  105.6 0.0 copy-done.2
  105.7 0.3 convert_reduce_fusion
  106.0 0.1 fusion.21
  106.1 0.1 pad_maximum_fusion.3.origin_ref
  106.2 0.0 copy-done.3
  106.2 0.1 copy.19
  106.3 0.1 reshape.32.coeffs_ref
  106.4 0.0 collective-permute-done
  106.4 0.0 collective-permute-done.1
  106.4 0.1 pad_maximum_fusion.2
  106.5 2.3 %collective-permute-start.2 = (bf16[15,542]{1,0:T(8,128)(2,1)S(1)}, bf16[15,542]{1,0:T(8,128)(2,1)S(1)}, u32[]{:S(2)}, u32[]{:S(2)}) collective-permute-start(bf16[15,542]{1,0:T(8,128)(2,1)S(1)} %get-tuple-element.5), channel_id=1, source_target_pairs={{0,1},{1,2},{2,3},{4,5},{5,6},{6,7},{8,9},{9,10},{10,11},{12,13},{... | collective-permute-start | bytes 48788 | tf_op jit(solution)/shard_map/ppermute | solution.py:26
  108.8 1.3 collective-permute-start.3
  110.1 0.0 all-to-all-done
  110.1 7.9 %broadcast_in_dim.2.high_ref = bf16[16384,128]{1,0:T(8,128)(2,1)S(1)} broadcast(bf16[16384]{0:T(1024)(128)(2,1)S(1)} %get-tuple-element.9), dimensions={0} | broadcast | bytes 4227072 | tf_op jit(solution)/shard_map/broadcast_in_dim | solution.py:130
  118.0 12.2 %shard_map.73 = bf16[128,16,128]{2,1,0:T(8,128)(2,1)} custom-call(f32[8,1,2048]{2,1,0:T(1,128)S(1)} %bitcast.23, bf16[16384,128]{1,0:T(8,128)(2,1)S(1)} %broadcast_in_dim.2.high_ref, bf16[16384,128]{1,0:T(8,128)(2,1)} %bitcast.6.rows_ref), custom_call_target="tpu_custom_call" | custom-call | flops 8600000512 | bytes 9000000 | tf_op jit(solution)/shard_map/pallas_call | solution.py:131
  130.2 7.9 %all-to-all-start.1 = ((bf16[128,16,128]{2,1,0:T(8,128)(2,1)}), bf16[128,16,128]{2,1,0:T(8,128)(2,1)S(1)}, u32[]{:S(2)}, u32[]{:S(2)}) async-start(bf16[128,16,128]{2,1,0:T(8,128)(2,1)} %shard_map.73), calls=%async_computation.1 | async-start | bytes 1048576 | tf_op jit(solution)/shard_map/all_to_all | solution.py:156
  138.1 0.0 collective-permute-done.2
  138.2 0.0 collective-permute-done.3
  138.2 0.5 fusion.9.padded_ref
  138.7 11.4 %shard_map.74 = f32[512,512]{1,0:T(8,128)S(1)} custom-call(f32[27]{0:T(128)S(1)} %reshape.32.coeffs_ref, f32[2]{0:T(128)S(1)} %pad_maximum_fusion.3.origin_ref, bf16[544,640]{1,0:T(8,128)(2,1)S(1)} %fusion.9.padded_ref, f32[16,256]{1,0:T(8,128)S(1)} %get-tuple-element.12.rows_ref, f32[16,256]{1,0:T(8,128)S(1)} %get-tuple-element.11.cols_ref), custom_call_target="tpu_custom_call" | custom-call | flops 3000000000 | bytes 2000000 | tf_op jit(solution)/shard_map/pallas_call | solution.py:88
  150.1 1.8 %all-to-all-done.1 = bf16[128,16,128]{2,1,0:T(8,128)(2,1)S(1)} async-done(((bf16[128,16,128]{2,1,0:T(8,128)(2,1)}), bf16[128,16,128]{2,1,0:T(8,128)(2,1)S(1)}, u32[]{:S(2)}, u32[]{:S(2)}) %all-to-all-start.1) | async-done | bytes 524320 | tf_op jit(solution)/shard_map/all_to_all | solution.py:156
  151.9 0.1 convert_multiply_fusion
  152.0 0.2 copy.18
  152.2 1.0 fusion.6
  (4 shorter events, 0.0 us)
Async XLA Ops:
  6.9 12.0 %copy-start = (bf16[512,512]{1,0:T(8,128)(2,1)S(1)}, bf16[512,512]{1,0:T(8,128)(2,1)}, u32[]{:S(2)}) copy-start(bf16[512,512]{1,0:T(8,128)(2,1)} %param.10) | copy-start | bytes 1572868
  6.9 17.6 %copy-start.4 = (s32[128]{0:T(128)S(1)}, s32[128]{0:T(128)}, u32[]{:S(2)}) copy-start(s32[128]{0:T(128)} %param.9) | copy-start | bytes 1540
  6.9 17.6 %copy-start.5 = (s32[128,1]{0,1:T(1,128)S(1)}, s32[128,1]{0,1:T(1,128)}, u32[]{:S(2)}) copy-start(s32[128,1]{0,1:T(1,128)} %param.8) | copy-start | bytes 1540
  6.9 98.8 %copy-start.1 = (bf16[9,31]{1,0:T(8,128)(2,1)S(1)}, bf16[9,31]{1,0:T(8,128)(2,1)}, u32[]{:S(2)}) copy-start(bf16[9,31]{1,0:T(8,128)(2,1)} %param.12) | copy-start | bytes 1678
  6.9 98.8 %copy-start.2 = (bf16[9,31]{1,0:T(8,128)(2,1)S(1)}, bf16[9,31]{1,0:T(8,128)(2,1)}, u32[]{:S(2)}) copy-start(bf16[9,31]{1,0:T(8,128)(2,1)} %param.11) | copy-start | bytes 1678
  6.9 99.3 %copy-start.3 = (f32[9,3]{0,1:T(4,128)S(1)}, f32[9,3]{0,1:T(4,128)}, u32[]{:S(2)}) copy-start(f32[9,3]{0,1:T(4,128)} %param.13) | copy-start | bytes 328
  6.9 103.2 %all-to-all-start = ((bf16[128,128,128]{2,0,1:T(8,128)(2,1)}), bf16[128,128,128]{2,0,1:T(8,128)(2,1)}, u32[]{:S(2)}, u32[]{:S(2)}) async-start(bf16[128,128,128]{2,0,1:T(8,128)(2,1)} %copy.17), calls=%async_computation | async-start | bytes 8388608 | tf_op jit(solution)/shard_map/all_to_all | solution.py:149
  19.0 87.4 %collective-permute-start = (bf16[512,15]{1,0:T(8,128)(2,1)S(1)}, bf16[512,15]{1,0:T(8,128)(2,1)S(1)}, u32[]{:S(2)}, u32[]{:S(2)}) collective-permute-start(bf16[512,15]{1,0:T(8,128)(2,1)S(1)} %get-tuple-element.7), channel_id=1, source_target_pairs={{0,4},{4,8},{8,12},{12,16},{16,20},{20,24},{24,28},{28,32},{32,36}... | collective-permute-start | bytes 46088 | tf_op jit(solution)/shard_map/ppermute | solution.py:26
  22.5 83.9 %collective-permute-start.1 = (bf16[512,15]{1,0:T(8,128)(2,1)S(1)}, bf16[512,15]{1,0:T(8,128)(2,1)S(1)}, u32[]{:S(2)}, u32[]{:S(2)}) collective-permute-start(bf16[512,15]{1,0:T(8,128)(2,1)S(1)} %get-tuple-element.8), channel_id=1, source_target_pairs={{4,0},{8,4},{12,8},{16,12},{20,16},{24,20},{28,24},{32,28},{36,32}... | collective-permute-start | bytes 46088 | tf_op jit(solution)/shard_map/ppermute | solution.py:26
  106.5 31.6 %collective-permute-start.2 = (bf16[15,542]{1,0:T(8,128)(2,1)S(1)}, bf16[15,542]{1,0:T(8,128)(2,1)S(1)}, u32[]{:S(2)}, u32[]{:S(2)}) collective-permute-start(bf16[15,542]{1,0:T(8,128)(2,1)S(1)} %get-tuple-element.5), channel_id=1, source_target_pairs={{0,1},{1,2},{2,3},{4,5},{5,6},{6,7},{8,9},{9,10},{10,11},{12,13},{... | collective-permute-start | bytes 48788 | tf_op jit(solution)/shard_map/ppermute | solution.py:26
  108.8 29.4 %collective-permute-start.3 = (bf16[15,542]{1,0:T(8,128)(2,1)S(1)}, bf16[15,542]{1,0:T(8,128)(2,1)S(1)}, u32[]{:S(2)}, u32[]{:S(2)}) collective-permute-start(bf16[15,542]{1,0:T(8,128)(2,1)S(1)} %get-tuple-element.6), channel_id=1, source_target_pairs={{1,0},{2,1},{3,2},{5,4},{6,5},{7,6},{9,8},{10,9},{11,10},{13,12},{... | collective-permute-start | bytes 48788 | tf_op jit(solution)/shard_map/ppermute | solution.py:26
  130.2 21.7 %all-to-all-start.1 = ((bf16[128,16,128]{2,1,0:T(8,128)(2,1)}), bf16[128,16,128]{2,1,0:T(8,128)(2,1)S(1)}, u32[]{:S(2)}, u32[]{:S(2)}) async-start(bf16[128,16,128]{2,1,0:T(8,128)(2,1)} %shard_map.73), calls=%async_computation.1 | async-start | bytes 1048576 | tf_op jit(solution)/shard_map/all_to_all | solution.py:156
where the time goes:
time: 154 us; the launch traced here: 153 us
  blocking collectives  81.1 us (53%)
  starting transfers between devices  28.9 us (19%)
  Pallas kernels  23.6 us (15%)
  local copies, waits for them, and re-layouts  15.3 us (10%)
  other arithmetic  2.3 us (1%)
  waiting for transfers between devices  1.77 us (1%)
    all_gather x1, blocking collectives, body(): keys = lax.all_gather(dest[:, 0] * 16 + slot, AXES, axis=0, tiled=True)  81.1 us
    pallas_call x1, Pallas kernels, merged(): pl.pallas_call(merge_kernel, grid=(steps,), out_shape=jax.ShapeDtypeStruc...  12.2 us
    all_to_all x1, starting transfers between devices, body(): lax.all_to_all(blocks, AXES, split_axis=1, concat_axis=0, tiled=True)  12 us
    pallas_call x1, Pallas kernels, model_of(): pl.pallas_call(model_kernel, out_shape=jax.ShapeDtypeStruct((EXTENT, EXTE...  11.4 us
    ppermute x4, starting transfers between devices, edge_shift(): return lax.ppermute(cells, axis, pairs)  9.01 us
    all_to_all x1, starting transfers between devices, body(): lax.all_to_all(sums, AXES, split_axis=0, concat_axis=0, tiled=True)  7.93 us
    broadcast_in_dim x1, local copies, waits for them, and re-layouts, merged(): jnp.broadcast_to((keys // 8 % 2).astype(jnp.bfloat16)[:, None], (count, TB))  7.91 us
    unnamed x14, local copies, waits for them, and re-layouts  6.97 us
  transfers between devices with their start and end apart: 6, of which 1 were waited for; matrix products, arithmetic and copies ran while one was open for 6% of the time, Pallas kernels for 15%

commit v1 on v0

--- a/solution.py
+++ b/solution.py
@@ -14,7 +14,10 @@
 TB = 128
 EXTENT = GRID * TB
 AXES = ("col", "row")
-STEP = 2048
+CHUNK = 16
+PARTS = TB // CHUNK
+DEPTH = 512
+VMEM_LIMIT = 56 << 20
 
 
 def edge_shift(cells, axis, up):
@@ -100,62 +103,140 @@
     )(coeffs.reshape(-1), origin, padded, taps_rows, taps_cols)
 
 
-def merge_kernel(keys_ref, high_ref, rows_ref, out_ref, acc):
-    step = pl.program_id(0)
-
-    @pl.when(step == 0)
-    def _():
-        acc[...] = jnp.zeros_like(acc)
-
-    upper = rows_ref[...] * high_ref[...]
-    lower = rows_ref[...] - upper
-    spread = jnp.concatenate([lower, upper], axis=1)
-    keys = keys_ref[0]
-    marks = lax.broadcasted_iota(jnp.int32, (256, STEP), 0).astype(jnp.bfloat16)
-    for part in range(4):
-        wanted = (keys - float(part * 256)).astype(jnp.bfloat16)
-        chosen = jnp.where(marks == wanted, jnp.bfloat16(1), jnp.bfloat16(0))
-        acc[part * 256:(part + 1) * 256, :] += jnp.dot(chosen, spread, preferred_element_type=jnp.float32)
-
-    @pl.when(step == pl.num_programs(0) - 1)
-    def _():
-        whole = acc[...].reshape(TB, 8, 2 * TB)
-        out_ref[...] = jnp.concatenate([whole[:, :, :TB], whole[:, :, TB:]], axis=1).astype(jnp.bfloat16)
-
-
-def merged(keys, rows):
-    count = keys.shape[0]
-    steps = count // STEP
-    places = ((keys // 16) * 8 + keys % 8).astype(jnp.float32).reshape(steps, 1, STEP)
-    high = jnp.broadcast_to(((keys // 8) % 2).astype(jnp.bfloat16)[:, None], (count, TB))
+def turn_kernel(dest_ref, slot_ref, blocks_ref, out_ref, loaded, swapped, ready, arriving, leaving):
+    arrivals = []
+    for k in range(PARTS):
+        part = pl.ds(k * CHUNK, CHUNK)
+        arrivals.append(pltpu.make_async_copy(blocks_ref.at[part], loaded.at[part], arriving.at[k]))
+        arrivals[k].start()
+    dests = dest_ref[...].astype(jnp.float32)
+    slots = slot_ref[...].astype(jnp.float32)
+    ranked = dests * float(TB) + lax.broadcasted_iota(jnp.int32, (1, TB), 1).astype(jnp.float32)
+    across = jnp.broadcast_to(ranked, (TB, TB))
+    place = jnp.where(across.T < across, 1.0, 0.0).sum(axis=0, keepdims=True)
+    down = lax.broadcasted_iota(jnp.int32, (TB, TB), 0).astype(jnp.float32)
+    order = jnp.where(down == place, 1.0, 0.0).astype(jnp.bfloat16)
+    pair = jnp.concatenate([dests, slots, jnp.zeros((14, TB), jnp.float32)], axis=0).astype(jnp.bfloat16)
+    labels = lax.dot_general(
+        pair, order, (((1,), (1,)), ((), ())), preferred_element_type=jnp.float32
+    ).astype(jnp.bfloat16)[:8]
+    for k in range(PARTS):
+        arrivals[k].wait()
+        part = pl.ds(k * CHUNK, CHUNK)
+        swapped[:, part, :] = jnp.swapaxes(loaded[part], 0, 1)
+    departures = []
+    for k in range(PARTS):
+        for r in range(k * CHUNK, (k + 1) * CHUNK):
+            ready[r, :TB, :] = jnp.dot(
+                order, swapped[r], preferred_element_type=jnp.float32
+            ).astype(jnp.bfloat16)
+            ready[r, TB:, :] = labels
+        part = pl.ds(k * CHUNK, CHUNK)
+        departures.append(pltpu.make_async_copy(ready.at[part], out_ref.at[part], leaving.at[k]))
+        departures[k].start()
+    for k in range(PARTS):
+        departures[k].wait()
+
+
+def turned(blocks, dest, slot):
+    label = pl.BlockSpec(memory_space=pltpu.VMEM)
+    far = pl.BlockSpec(memory_space=pl.ANY)
+    return pl.pallas_call(
+        turn_kernel,
+        out_shape=jax.ShapeDtypeStruct((TB, TB + 8, TB), jnp.bfloat16),
+        in_specs=[label, label, far],
+        out_specs=far,
+        scratch_shapes=[
+            pltpu.VMEM((TB, TB, TB), jnp.bfloat16),
+            pltpu.VMEM((TB, TB, TB), jnp.bfloat16),
+            pltpu.VMEM((TB, TB + 8, TB), jnp.bfloat16),
+            pltpu.SemaphoreType.DMA((PARTS,)),
+            pltpu.SemaphoreType.DMA((PARTS,)),
+        ],
+        compiler_params=pltpu.CompilerParams(vmem_limit_bytes=VMEM_LIMIT),
+        cost_estimate=pl.CostEstimate(flops=600_000_000, bytes_accessed=8_700_000, transcendentals=0),
+    )(dest.reshape(1, TB), slot.reshape(1, TB), blocks)
+
+
+def merge_kernel(arrived_ref, out_ref, keys_ref, labels, rows, acc, spread, labels_sem, rows_sem):
+    named = pltpu.make_async_copy(arrived_ref.at[:, pl.ds(TB, 8), :], labels, labels_sem)
+    named.start()
+    arrivals = []
+    for k in range(PARTS):
+        part = pl.ds(k * CHUNK, CHUNK)
+        arrivals.append(pltpu.make_async_copy(arrived_ref.at[:, part, :], rows.at[k], rows_sem.at[k]))
+        arrivals[k].start()
+    acc[...] = jnp.zeros_like(acc)
+    lanes = lax.broadcasted_iota(jnp.int32, (TB, TB), 1) // CHUNK
+    owners = lax.broadcasted_iota(jnp.int32, (TB, TB), 0) % 8
+    named.wait()
+    tags = labels[...].astype(jnp.float32)
+    keys = tags[:, 0, :] * 16.0 + tags[:, 1, :]
+    keys_ref[...] = keys
+    skewed = pltpu.roll(keys, 0, 1, stride=CHUNK, stride_axis=0)
+    for k in range(PARTS):
+        shifted = pltpu.roll(skewed, (TB - k * CHUNK) % TB, 1)
+        lines = jnp.where(lanes == owners, shifted, 0.0).reshape(16, 8, TB).sum(axis=1)
+        dests = jnp.floor(lines * (1.0 / 16.0))
+        slots = lines - 16.0 * dests
+        high = jnp.where(slots >= 8.0, 1.0, 0.0)
+        places = dests * 8.0 + slots - 8.0 * high - float(k * 64)
+        high_down = high.T
+        arrivals[k].wait()
+        for g in range(16):
+            taken = rows[k, g * 8:(g + 1) * 8].reshape(TB, TB)
+            mask = jnp.broadcast_to(high_down[:, g:g + 1], (TB, TB)).astype(jnp.bfloat16)
+            upper = taken * mask
+            spread[k % 2, g * TB:(g + 1) * TB, TB:] = upper
+            spread[k % 2, g * TB:(g + 1) * TB, :TB] = taken - upper
+        line = jnp.concatenate([places[g:g + 1, :] for g in range(16)], axis=1)
+        for first, size in ((0, 256), (256, 256), (512, 64)):
+            marks = lax.broadcasted_iota(jnp.int32, (size, DEPTH), 0).astype(jnp.bfloat16)
+            wanted = (line - float(first)).astype(jnp.bfloat16)
+            total = acc[k * 64 + first:k * 64 + first + size, :]
+            for q in range(0, 16 * TB, DEPTH):
+                chosen = jnp.where(marks == wanted[:, q:q + DEPTH], jnp.bfloat16(1), jnp.bfloat16(0))
+                total = total + jnp.dot(chosen, spread[k % 2, q:q + DEPTH, :], preferred_element_type=jnp.float32)
+            acc[k * 64 + first:k * 64 + first + size, :] = total
+    whole = acc[...].reshape(TB, 8, 2 * TB)
+    out_ref[...] = jnp.concatenate([whole[:, :, :TB], whole[:, :, TB:]], axis=1).astype(jnp.bfloat16)
+
+
+def merged(arrived):
+    near = pl.BlockSpec(memory_space=pltpu.VMEM)
     return pl.pallas_call(
         merge_kernel,
-        grid=(steps,),
-        out_shape=jax.ShapeDtypeStruct((TB, 16, TB), jnp.bfloat16),
-        in_specs=[
-            pl.BlockSpec((1, 1, STEP), lambda k: (k, 0, 0)),
-            pl.BlockSpec((STEP, TB), lambda k: (k, 0)),
-            pl.BlockSpec((STEP, TB), lambda k: (k, 0)),
+        out_shape=(
+            jax.ShapeDtypeStruct((TB, 16, TB), jnp.bfloat16),
+            jax.ShapeDtypeStruct((TB, TB), jnp.float32),
+        ),
+        in_specs=[pl.BlockSpec(memory_space=pl.ANY)],
+        out_specs=(near, near),
+        scratch_shapes=[
+            pltpu.VMEM((TB, 8, TB), jnp.bfloat16),
+            pltpu.VMEM((PARTS, TB, CHUNK, TB), jnp.bfloat16),
+            pltpu.VMEM((1024, 2 * TB), jnp.float32),
+            pltpu.VMEM((2, 16 * TB, 2 * TB), jnp.bfloat16),
+            pltpu.SemaphoreType.DMA,
+            pltpu.SemaphoreType.DMA((PARTS,)),
         ],
-        out_specs=pl.BlockSpec((TB, 16, TB), lambda k: (0, 0, 0)),
-        scratch_shapes=[pltpu.VMEM((1024, 2 * TB), jnp.float32)],
-        compiler_params=pltpu.CompilerParams(vmem_limit_bytes=24 << 20),
-        cost_estimate=pl.CostEstimate(flops=8_600_000_000, bytes_accessed=9_000_000, transcendentals=0),
-    )(places, high, rows)
+        compiler_params=pltpu.CompilerParams(vmem_limit_bytes=VMEM_LIMIT),
+        cost_estimate=pl.CostEstimate(flops=5_000_000_000, bytes_accessed=5_000_000, transcendentals=0),
+    )(arrived)
 
 
 def body(blocks, dest, slot, template, kern_rows, kern_cols, coeffs):
-    keys = lax.all_gather(dest[:, 0] * 16 + slot, AXES, axis=0, tiled=True)
-    rows = lax.all_to_all(blocks, AXES, split_axis=1, concat_axis=0, tiled=True).reshape(-1, TB)
+    parcels = turned(blocks, dest, slot)
+    arrived = lax.all_to_all(parcels, AXES, split_axis=0, concat_axis=0, tiled=True)
     model = model_of(with_halo(template), kern_rows, kern_cols, coeffs)
+    sums, keys = merged(arrived)
+    gathered = lax.all_to_all(sums, AXES, split_axis=0, concat_axis=0, tiled=True)
     mine = lax.axis_index("col") * 4 + lax.axis_index("row")
-    tiles = mine * 16 + jnp.arange(16, dtype=jnp.int32)
-    counts = (keys[None, :] == tiles[:, None]).astype(jnp.float32).sum(axis=1)
+    tiles = (mine * 16 + jnp.arange(16, dtype=jnp.int32)).astype(jnp.float32)
+    counts = (keys[None] == tiles[:, None, None]).astype(jnp.float32).sum(axis=(1, 2))
     inverse = 1.0 / jnp.maximum(counts, 1.0)
-    sums = merged(keys, rows)
-    arrived = lax.all_to_all(sums, AXES, split_axis=0, concat_axis=0, tiled=True)
     science = (
-        (arrived.astype(jnp.float32) * inverse[None, :, None])
+        (gathered.astype(jnp.float32) * inverse[None, :, None])
         .reshape(TB, GRID, GRID, TB)
         .transpose(1, 0, 2, 3)
         .reshape(EXTENT, EXTENT)

time: 154 us -> 113 us (0.73)
  blocking collectives: 81.1 us -> 0 us
  waiting for transfers between devices: 1.77 us -> 50.1 us
  local copies, waits for them, and re-layouts: 15.3 us -> 0.5 us
  Pallas kernels: 23.6 us -> 28.2 us
  starting transfers between devices: 28.9 us -> 31.5 us
    all_gather x1 -> x0, blocking collectives: 81.1 us -> none  [body(): keys = lax.all_gather(dest[:, 0] * 16 + slot, AXES, axis=0, tiled=True)]
    ppermute x4, waiting for transfers between devices: 0.01 us -> 48.1 us  [edge_shift(): return lax.ppermute(cells, axis, pairs)]
    broadcast_in_dim x1 -> x0, local copies, waits for them, and re-layouts: 7.91 us -> none  [merged(): jnp.broadcast_to((keys // 8 % 2).astype(jnp.bfloat16)[:, None], (count, TB))]
    unnamed x14 -> x11, local copies, waits for them, and re-layouts: 6.97 us -> 0.12 us
    pallas_call x1 -> x2, Pallas kernels: 12.2 us -> 16.8 us  [the longest x1 11.3 us: merged(): pl.pallas_call(merge_kernel, out_shape=(jax.ShapeDtypeStruct((TB, 16, TB)...]
    all_to_all x1, starting transfers between devices: 7.93 us -> 9.8 us  [body(): lax.all_to_all(sums, AXES, split_axis=0, concat_axis=0, tiled=True)]
  transfers between devices with their start and end apart: 6 -> 6, of which waited for: 1 -> 4; matrix products, arithmetic and copies ran while one was open for 6% -> 1% of each run, Pallas kernels for 15% -> 10%
where the time goes in v1:
time: 113 us
  waiting for transfers between devices  50.1 us (44%)
  starting transfers between devices  31.5 us (28%)
  Pallas kernels  28.2 us (25%)
  other arithmetic  2.14 us (2%)
    ppermute x4, waiting for transfers between devices, edge_shift(): return lax.ppermute(cells, axis, pairs)  48.1 us
    all_to_all x1, starting transfers between devices, body(): lax.all_to_all(parcels, AXES, split_axis=0, concat_axis=0, tiled=True)  11.9 us
    pallas_call x1, Pallas kernels, model_of(): pl.pallas_call(model_kernel, out_shape=jax.ShapeDtypeStruct((EXTENT, EXTE...  11.4 us
    pallas_call x1, Pallas kernels, merged(): pl.pallas_call(merge_kernel, out_shape=(jax.ShapeDtypeStruct((TB, 16, TB)...  11.3 us
    ppermute x4, starting transfers between devices, edge_shift(): return lax.ppermute(cells, axis, pairs)  9.84 us
    all_to_all x1, starting transfers between devices, body(): lax.all_to_all(sums, AXES, split_axis=0, concat_axis=0, tiled=True)  9.8 us
    pallas_call x1, Pallas kernels, turned(): pl.pallas_call(turn_kernel, out_shape=jax.ShapeDtypeStruct((TB, TB + 8, T...  5.44 us
  transfers between devices with their start and end apart: 6, of which 4 were waited for; matrix products, arithmetic and copies ran while one was open for 1% of the time, Pallas kernels for 10%

profile of v1, /device:TPU:1, one launch (start us, length us, event | category | flops | bytes accessed | tf_op | source)
XLA Modules:
  0.0 112.7 jit_solution(12158757479981936703)
XLA Ops:
  0.0 5.4 %shard_map.73 = bf16[128,136,128]{2,1,0:T(8,128)(2,1)} custom-call(s32[1,128]{1,0:T(1,128)} %bitcast.14, s32[1,128]{1,0:T(1,128)} %bitcast.15, bf16[128,128,128]{2,1,0:T(8,128)(2,1)} %blocks_ref.1), custom_call_target="tpu_custom_call" | custom-call | flops 600000000 | bytes 8700000 | tf_op jit(solution)/shard_map/pallas_call | solution.py:144
  5.4 0.0 copy-start
  5.5 0.0 copy-start.2
  5.5 0.0 copy-start.3
  5.5 11.9 %all-to-all-start = ((bf16[128,136,128]{2,1,0:T(8,128)(2,1)}), bf16[128,136,128]{2,1,0:T(8,128)(2,1)}, u32[]{:S(2)}, u32[]{:S(2)}) async-start(bf16[128,136,128]{2,1,0:T(8,128)(2,1)} %shard_map.73), calls=%async_computation | async-start | bytes 8912896 | tf_op jit(solution)/shard_map/all_to_all | solution.py:230
  17.4 0.0 copy-done
  17.4 0.0 copy-start.4
  17.4 0.1 fusion.16
  17.5 3.5 %collective-permute-start = (bf16[512,15]{1,0:T(8,128)(2,1)S(1)}, bf16[512,15]{1,0:T(8,128)(2,1)S(1)}, u32[]{:S(2)}, u32[]{:S(2)}) collective-permute-start(bf16[512,15]{1,0:T(8,128)(2,1)S(1)} %get-tuple-element.11), channel_id=1, source_target_pairs={{0,4},{4,8},{8,12},{12,16},{16,20},{20,24},{24,28},{28,32},{32,36}... | collective-permute-start | bytes 46088 | tf_op jit(solution)/shard_map/ppermute | solution.py:29
  21.1 1.9 %collective-permute-start.1 = (bf16[512,15]{1,0:T(8,128)(2,1)S(1)}, bf16[512,15]{1,0:T(8,128)(2,1)S(1)}, u32[]{:S(2)}, u32[]{:S(2)}) collective-permute-start(bf16[512,15]{1,0:T(8,128)(2,1)S(1)} %get-tuple-element.12), channel_id=1, source_target_pairs={{4,0},{8,4},{12,8},{16,12},{20,16},{24,20},{28,24},{32,28},{36,32}... | collective-permute-start | bytes 46088 | tf_op jit(solution)/shard_map/ppermute | solution.py:29
  23.0 0.0 copy-done.2
  23.0 0.0 copy-done.3
  23.1 42.9 %collective-permute-done = bf16[512,15]{1,0:T(8,128)(2,1)S(1)} collective-permute-done((bf16[512,15]{1,0:T(8,128)(2,1)S(1)}, bf16[512,15]{1,0:T(8,128)(2,1)S(1)}, u32[]{:S(2)}, u32[]{:S(2)}) %collective-permute-start) | collective-permute-done | bytes 15392 | tf_op jit(solution)/shard_map/ppermute | solution.py:29
  66.0 2.2 %collective-permute-done.1 = bf16[512,15]{1,0:T(8,128)(2,1)S(1)} collective-permute-done((bf16[512,15]{1,0:T(8,128)(2,1)S(1)}, bf16[512,15]{1,0:T(8,128)(2,1)S(1)}, u32[]{:S(2)}, u32[]{:S(2)}) %collective-permute-start.1) | collective-permute-done | bytes 15392 | tf_op jit(solution)/shard_map/ppermute | solution.py:29
  68.2 0.1 pad_maximum_fusion.2
  68.3 3.1 %collective-permute-start.2 = (bf16[15,542]{1,0:T(8,128)(2,1)S(1)}, bf16[15,542]{1,0:T(8,128)(2,1)S(1)}, u32[]{:S(2)}, u32[]{:S(2)}) collective-permute-start(bf16[15,542]{1,0:T(8,128)(2,1)S(1)} %get-tuple-element.9), channel_id=1, source_target_pairs={{0,1},{1,2},{2,3},{4,5},{5,6},{6,7},{8,9},{9,10},{10,11},{12,13},{... | collective-permute-start | bytes 48788 | tf_op jit(solution)/shard_map/ppermute | solution.py:29
  71.4 1.3 %collective-permute-start.3 = (bf16[15,542]{1,0:T(8,128)(2,1)S(1)}, bf16[15,542]{1,0:T(8,128)(2,1)S(1)}, u32[]{:S(2)}, u32[]{:S(2)}) collective-permute-start(bf16[15,542]{1,0:T(8,128)(2,1)S(1)} %get-tuple-element.10), channel_id=1, source_target_pairs={{1,0},{2,1},{3,2},{5,4},{6,5},{7,6},{9,8},{10,9},{11,10},{13,12},{... | collective-permute-start | bytes 48788 | tf_op jit(solution)/shard_map/ppermute | solution.py:29
  72.7 0.1 pad_maximum_fusion.3.origin_ref
  72.8 0.0 copy-done.4
  72.8 0.1 copy.13
  72.9 0.1 reshape.29.coeffs_ref
  73.0 0.0 collective-permute-done.2
  73.0 3.0 %collective-permute-done.3 = bf16[15,542]{1,0:T(8,128)(2,1)S(1)} collective-permute-done((bf16[15,542]{1,0:T(8,128)(2,1)S(1)}, bf16[15,542]{1,0:T(8,128)(2,1)S(1)}, u32[]{:S(2)}, u32[]{:S(2)}) %collective-permute-start.3) | collective-permute-done | bytes 16292 | tf_op jit(solution)/shard_map/ppermute | solution.py:29
  75.9 0.5 fusion.9.padded_ref
  76.5 0.0 all-to-all-done.arrived_ref
  76.5 11.3 %shard_map.74 = (bf16[128,16,128]{2,1,0:T(8,128)(2,1)}, f32[128,128]{1,0:T(8,128)}) custom-call(bf16[128,136,128]{2,1,0:T(8,128)(2,1)} %all-to-all-done.arrived_ref), custom_call_target="tpu_custom_call" | custom-call | flops 5000000000 | bytes 5000000 | tf_op jit(solution)/shard_map/pallas_call | solution.py:207
  87.8 9.8 %all-to-all-start.1 = ((bf16[128,16,128]{2,1,0:T(8,128)(2,1)}), bf16[128,16,128]{2,1,0:T(8,128)(2,1)S(1)}, u32[]{:S(2)}, u32[]{:S(2)}) async-start(bf16[128,16,128]{2,1,0:T(8,128)(2,1)} %get-tuple-element.7), calls=%async_computation.1 | async-start | bytes 1048576 | tf_op jit(solution)/shard_map/all_to_all | solution.py:233
  97.6 0.0 copy-start.1
  97.6 11.4 %shard_map.75 = f32[512,512]{1,0:T(8,128)S(1)} custom-call(f32[27]{0:T(128)S(1)} %reshape.29.coeffs_ref, f32[2]{0:T(128)S(1)} %pad_maximum_fusion.3.origin_ref, bf16[544,640]{1,0:T(8,128)(2,1)S(1)} %fusion.9.padded_ref, f32[16,256]{1,0:T(8,128)S(1)} %get-tuple-element.14.rows_ref, f32[16,256]{1,0:T(8,128)S(1)} %get-tuple-element.13.cols_ref), custom_call_target="tpu_custom_call" | custom-call | flops 3000000000 | bytes 2000000 | tf_op jit(solution)/shard_map/pallas_call | solution.py:91
  109.1 0.0 copy-done.1
  109.1 0.3 convert_reduce_fusion
  109.4 2.0 %all-to-all-done.1 = bf16[128,16,128]{2,1,0:T(8,128)(2,1)S(1)} async-done(((bf16[128,16,128]{2,1,0:T(8,128)(2,1)}), bf16[128,16,128]{2,1,0:T(8,128)(2,1)S(1)}, u32[]{:S(2)}, u32[]{:S(2)}) %all-to-all-start.1) | async-done | bytes 524320 | tf_op jit(solution)/shard_map/all_to_all | solution.py:233
  111.4 0.1 convert_multiply_fusion
  111.5 0.2 copy.12
  111.7 1.0 fusion.6
  (3 shorter events, 0.0 us)
Async XLA Ops:
  5.4 11.9 %copy-start = (bf16[512,512]{1,0:T(8,128)(2,1)S(1)}, bf16[512,512]{1,0:T(8,128)(2,1)}, u32[]{:S(2)}) copy-start(bf16[512,512]{1,0:T(8,128)(2,1)} %param.10) | copy-start | bytes 1572868
  5.5 17.5 %copy-start.2 = (bf16[9,31]{1,0:T(8,128)(2,1)S(1)}, bf16[9,31]{1,0:T(8,128)(2,1)}, u32[]{:S(2)}) copy-start(bf16[9,31]{1,0:T(8,128)(2,1)} %param.12) | copy-start | bytes 1678
  5.5 17.5 %copy-start.3 = (bf16[9,31]{1,0:T(8,128)(2,1)S(1)}, bf16[9,31]{1,0:T(8,128)(2,1)}, u32[]{:S(2)}) copy-start(bf16[9,31]{1,0:T(8,128)(2,1)} %param.11) | copy-start | bytes 1678
  5.5 71.0 %all-to-all-start = ((bf16[128,136,128]{2,1,0:T(8,128)(2,1)}), bf16[128,136,128]{2,1,0:T(8,128)(2,1)}, u32[]{:S(2)}, u32[]{:S(2)}) async-start(bf16[128,136,128]{2,1,0:T(8,128)(2,1)} %shard_map.73), calls=%async_computation | async-start | bytes 8912896 | tf_op jit(solution)/shard_map/all_to_all | solution.py:230
  17.4 55.4 %copy-start.4 = (f32[9,3]{0,1:T(4,128)S(1)}, f32[9,3]{0,1:T(4,128)}, u32[]{:S(2)}) copy-start(f32[9,3]{0,1:T(4,128)} %param.13) | copy-start | bytes 328
  17.5 48.5 %collective-permute-start = (bf16[512,15]{1,0:T(8,128)(2,1)S(1)}, bf16[512,15]{1,0:T(8,128)(2,1)S(1)}, u32[]{:S(2)}, u32[]{:S(2)}) collective-permute-start(bf16[512,15]{1,0:T(8,128)(2,1)S(1)} %get-tuple-element.11), channel_id=1, source_target_pairs={{0,4},{4,8},{8,12},{12,16},{16,20},{20,24},{24,28},{28,32},{32,36}... | collective-permute-start | bytes 46088 | tf_op jit(solution)/shard_map/ppermute | solution.py:29
  21.1 47.1 %collective-permute-start.1 = (bf16[512,15]{1,0:T(8,128)(2,1)S(1)}, bf16[512,15]{1,0:T(8,128)(2,1)S(1)}, u32[]{:S(2)}, u32[]{:S(2)}) collective-permute-start(bf16[512,15]{1,0:T(8,128)(2,1)S(1)} %get-tuple-element.12), channel_id=1, source_target_pairs={{4,0},{8,4},{12,8},{16,12},{20,16},{24,20},{28,24},{32,28},{36,32}... | collective-permute-start | bytes 46088 | tf_op jit(solution)/shard_map/ppermute | solution.py:29
  68.3 4.7 %collective-permute-start.2 = (bf16[15,542]{1,0:T(8,128)(2,1)S(1)}, bf16[15,542]{1,0:T(8,128)(2,1)S(1)}, u32[]{:S(2)}, u32[]{:S(2)}) collective-permute-start(bf16[15,542]{1,0:T(8,128)(2,1)S(1)} %get-tuple-element.9), channel_id=1, source_target_pairs={{0,1},{1,2},{2,3},{4,5},{5,6},{6,7},{8,9},{9,10},{10,11},{12,13},{... | collective-permute-start | bytes 48788 | tf_op jit(solution)/shard_map/ppermute | solution.py:29
  71.4 4.5 %collective-permute-start.3 = (bf16[15,542]{1,0:T(8,128)(2,1)S(1)}, bf16[15,542]{1,0:T(8,128)(2,1)S(1)}, u32[]{:S(2)}, u32[]{:S(2)}) collective-permute-start(bf16[15,542]{1,0:T(8,128)(2,1)S(1)} %get-tuple-element.10), channel_id=1, source_target_pairs={{1,0},{2,1},{3,2},{5,4},{6,5},{7,6},{9,8},{10,9},{11,10},{13,12},{... | collective-permute-start | bytes 48788 | tf_op jit(solution)/shard_map/ppermute | solution.py:29
  87.8 23.6 %all-to-all-start.1 = ((bf16[128,16,128]{2,1,0:T(8,128)(2,1)}), bf16[128,16,128]{2,1,0:T(8,128)(2,1)S(1)}, u32[]{:S(2)}, u32[]{:S(2)}) async-start(bf16[128,16,128]{2,1,0:T(8,128)(2,1)} %get-tuple-element.7), calls=%async_computation.1 | async-start | bytes 1048576 | tf_op jit(solution)/shard_map/all_to_all | solution.py:233
  97.6 11.4 %copy-start.1 = (f32[128,128]{1,0:T(8,128)S(1)}, f32[128,128]{1,0:T(8,128)}, u32[]{:S(2)}) copy-start(f32[128,128]{1,0:T(8,128)} %get-tuple-element.8) | copy-start | bytes 196612

commit v2 on v1

--- a/solution.py
+++ b/solution.py
@@ -175,6 +175,8 @@
     keys_ref[...] = keys
     skewed = pltpu.roll(keys, 0, 1, stride=CHUNK, stride_axis=0)
     for k in range(PARTS):
+        arrivals[k].wait()
+    for k in range(PARTS):
         shifted = pltpu.roll(skewed, (TB - k * CHUNK) % TB, 1)
         lines = jnp.where(lanes == owners, shifted, 0.0).reshape(16, 8, TB).sum(axis=1)
         dests = jnp.floor(lines * (1.0 / 16.0))
@@ -182,7 +184,6 @@
         high = jnp.where(slots >= 8.0, 1.0, 0.0)
         places = dests * 8.0 + slots - 8.0 * high - float(k * 64)
         high_down = high.T
-        arrivals[k].wait()
         for g in range(16):
             taken = rows[k, g * 8:(g + 1) * 8].reshape(TB, TB)
             mask = jnp.broadcast_to(high_down[:, g:g + 1], (TB, TB)).astype(jnp.bfloat16)
@@ -190,14 +191,16 @@
             spread[k % 2, g * TB:(g + 1) * TB, TB:] = upper
             spread[k % 2, g * TB:(g + 1) * TB, :TB] = taken - upper
         line = jnp.concatenate([places[g:g + 1, :] for g in range(16)], axis=1)
-        for first, size in ((0, 256), (256, 256), (512, 64)):
-            marks = lax.broadcasted_iota(jnp.int32, (size, DEPTH), 0).astype(jnp.bfloat16)
-            wanted = (line - float(first)).astype(jnp.bfloat16)
-            total = acc[k * 64 + first:k * 64 + first + size, :]
+        for first, size in ((0, 256), (256, 320)):
+            middle = size // 2
+            marks = (lax.broadcasted_iota(jnp.int32, (size, DEPTH), 0) - middle).astype(jnp.bfloat16)
+            wanted = (line - float(first + middle)).astype(jnp.bfloat16)
+            window = slice(k * 64 + first, k * 64 + first + size)
+            total = acc[window, :]
             for q in range(0, 16 * TB, DEPTH):
                 chosen = jnp.where(marks == wanted[:, q:q + DEPTH], jnp.bfloat16(1), jnp.bfloat16(0))
                 total = total + jnp.dot(chosen, spread[k % 2, q:q + DEPTH, :], preferred_element_type=jnp.float32)
-            acc[k * 64 + first:k * 64 + first + size, :] = total
+            acc[window, :] = total
     whole = acc[...].reshape(TB, 8, 2 * TB)
     out_ref[...] = jnp.concatenate([whole[:, :, :TB], whole[:, :, TB:]], axis=1).astype(jnp.bfloat16)
 

time: 113 us -> 111 us (0.982)
  Pallas kernels: 28.2 us -> 26.1 us
    pallas_call x1, Pallas kernels: 11.3 us -> 9.22 us  [merged(): pl.pallas_call(merge_kernel, out_shape=(jax.ShapeDtypeStruct((TB, 16, TB)...]
where the time goes in v2:
time: 111 us
  waiting for transfers between devices  50.1 us (45%)
  starting transfers between devices  31.5 us (28%)
  Pallas kernels  26.1 us (24%)
  other arithmetic  2.14 us (2%)
    ppermute x4, waiting for transfers between devices, edge_shift(): return lax.ppermute(cells, axis, pairs)  48.1 us
    all_to_all x1, starting transfers between devices, body(): lax.all_to_all(parcels, AXES, split_axis=0, concat_axis=0, tiled=True)  11.9 us
    pallas_call x1, Pallas kernels, model_of(): pl.pallas_call(model_kernel, out_shape=jax.ShapeDtypeStruct((EXTENT, EXTE...  11.4 us
    ppermute x4, starting transfers between devices, edge_shift(): return lax.ppermute(cells, axis, pairs)  9.84 us
    all_to_all x1, starting transfers between devices, body(): lax.all_to_all(sums, AXES, split_axis=0, concat_axis=0, tiled=True)  9.8 us
    pallas_call x1, Pallas kernels, merged(): pl.pallas_call(merge_kernel, out_shape=(jax.ShapeDtypeStruct((TB, 16, TB)...  9.22 us
    pallas_call x1, Pallas kernels, turned(): pl.pallas_call(turn_kernel, out_shape=jax.ShapeDtypeStruct((TB, TB + 8, T...  5.44 us
  transfers between devices with their start and end apart: 6, of which 4 were waited for; matrix products, arithmetic and copies ran while one was open for 1% of the time, Pallas kernels for 10%

profile of v2, /device:TPU:1, one launch (start us, length us, event | category | flops | bytes accessed | tf_op | source)
XLA Modules:
  0.0 110.6 jit_solution(4919217943883957400)
XLA Ops:
  0.0 5.4 %shard_map.73 = bf16[128,136,128]{2,1,0:T(8,128)(2,1)} custom-call(s32[1,128]{1,0:T(1,128)} %bitcast.14, s32[1,128]{1,0:T(1,128)} %bitcast.15, bf16[128,128,128]{2,1,0:T(8,128)(2,1)} %blocks_ref.1), custom_call_target="tpu_custom_call" | custom-call | flops 600000000 | bytes 8700000 | tf_op jit(solution)/shard_map/pallas_call | solution.py:144
  5.4 0.0 copy-start
  5.5 0.0 copy-start.2
  5.5 0.0 copy-start.3
  5.5 11.9 %all-to-all-start = ((bf16[128,136,128]{2,1,0:T(8,128)(2,1)}), bf16[128,136,128]{2,1,0:T(8,128)(2,1)}, u32[]{:S(2)}, u32[]{:S(2)}) async-start(bf16[128,136,128]{2,1,0:T(8,128)(2,1)} %shard_map.73), calls=%async_computation | async-start | bytes 8912896 | tf_op jit(solution)/shard_map/all_to_all | solution.py:233
  17.4 0.0 copy-done
  17.4 0.0 copy-start.4
  17.4 0.1 fusion.16
  17.5 3.5 %collective-permute-start = (bf16[512,15]{1,0:T(8,128)(2,1)S(1)}, bf16[512,15]{1,0:T(8,128)(2,1)S(1)}, u32[]{:S(2)}, u32[]{:S(2)}) collective-permute-start(bf16[512,15]{1,0:T(8,128)(2,1)S(1)} %get-tuple-element.11), channel_id=1, source_target_pairs={{0,4},{4,8},{8,12},{12,16},{16,20},{20,24},{24,28},{28,32},{32,36}... | collective-permute-start | bytes 46088 | tf_op jit(solution)/shard_map/ppermute | solution.py:29
  21.1 1.9 %collective-permute-start.1 = (bf16[512,15]{1,0:T(8,128)(2,1)S(1)}, bf16[512,15]{1,0:T(8,128)(2,1)S(1)}, u32[]{:S(2)}, u32[]{:S(2)}) collective-permute-start(bf16[512,15]{1,0:T(8,128)(2,1)S(1)} %get-tuple-element.12), channel_id=1, source_target_pairs={{4,0},{8,4},{12,8},{16,12},{20,16},{24,20},{28,24},{32,28},{36,32}... | collective-permute-start | bytes 46088 | tf_op jit(solution)/shard_map/ppermute | solution.py:29
  23.0 0.0 copy-done.2
  23.0 0.0 copy-done.3
  23.1 42.9 %collective-permute-done = bf16[512,15]{1,0:T(8,128)(2,1)S(1)} collective-permute-done((bf16[512,15]{1,0:T(8,128)(2,1)S(1)}, bf16[512,15]{1,0:T(8,128)(2,1)S(1)}, u32[]{:S(2)}, u32[]{:S(2)}) %collective-permute-start) | collective-permute-done | bytes 15392 | tf_op jit(solution)/shard_map/ppermute | solution.py:29
  66.0 2.2 %collective-permute-done.1 = bf16[512,15]{1,0:T(8,128)(2,1)S(1)} collective-permute-done((bf16[512,15]{1,0:T(8,128)(2,1)S(1)}, bf16[512,15]{1,0:T(8,128)(2,1)S(1)}, u32[]{:S(2)}, u32[]{:S(2)}) %collective-permute-start.1) | collective-permute-done | bytes 15392 | tf_op jit(solution)/shard_map/ppermute | solution.py:29
  68.2 0.1 pad_maximum_fusion.2
  68.3 3.1 %collective-permute-start.2 = (bf16[15,542]{1,0:T(8,128)(2,1)S(1)}, bf16[15,542]{1,0:T(8,128)(2,1)S(1)}, u32[]{:S(2)}, u32[]{:S(2)}) collective-permute-start(bf16[15,542]{1,0:T(8,128)(2,1)S(1)} %get-tuple-element.9), channel_id=1, source_target_pairs={{0,1},{1,2},{2,3},{4,5},{5,6},{6,7},{8,9},{9,10},{10,11},{12,13},{... | collective-permute-start | bytes 48788 | tf_op jit(solution)/shard_map/ppermute | solution.py:29
  71.4 1.3 %collective-permute-start.3 = (bf16[15,542]{1,0:T(8,128)(2,1)S(1)}, bf16[15,542]{1,0:T(8,128)(2,1)S(1)}, u32[]{:S(2)}, u32[]{:S(2)}) collective-permute-start(bf16[15,542]{1,0:T(8,128)(2,1)S(1)} %get-tuple-element.10), channel_id=1, source_target_pairs={{1,0},{2,1},{3,2},{5,4},{6,5},{7,6},{9,8},{10,9},{11,10},{13,12},{... | collective-permute-start | bytes 48788 | tf_op jit(solution)/shard_map/ppermute | solution.py:29
  72.7 0.1 pad_maximum_fusion.3.origin_ref
  72.8 0.0 copy-done.4
  72.8 0.1 copy.13
  72.9 0.1 reshape.29.coeffs_ref
  73.0 0.0 collective-permute-done.2
  73.0 3.0 %collective-permute-done.3 = bf16[15,542]{1,0:T(8,128)(2,1)S(1)} collective-permute-done((bf16[15,542]{1,0:T(8,128)(2,1)S(1)}, bf16[15,542]{1,0:T(8,128)(2,1)S(1)}, u32[]{:S(2)}, u32[]{:S(2)}) %collective-permute-start.3) | collective-permute-done | bytes 16292 | tf_op jit(solution)/shard_map/ppermute | solution.py:29
  75.9 0.5 fusion.9.padded_ref
  76.5 0.0 all-to-all-done.arrived_ref
  76.5 9.2 %shard_map.74 = (bf16[128,16,128]{2,1,0:T(8,128)(2,1)}, f32[128,128]{1,0:T(8,128)}) custom-call(bf16[128,136,128]{2,1,0:T(8,128)(2,1)} %all-to-all-done.arrived_ref), custom_call_target="tpu_custom_call" | custom-call | flops 5000000000 | bytes 5000000 | tf_op jit(solution)/shard_map/pallas_call | solution.py:210
  85.7 9.8 %all-to-all-start.1 = ((bf16[128,16,128]{2,1,0:T(8,128)(2,1)}), bf16[128,16,128]{2,1,0:T(8,128)(2,1)S(1)}, u32[]{:S(2)}, u32[]{:S(2)}) async-start(bf16[128,16,128]{2,1,0:T(8,128)(2,1)} %get-tuple-element.7), calls=%async_computation.1 | async-start | bytes 1048576 | tf_op jit(solution)/shard_map/all_to_all | solution.py:236
  95.5 0.0 copy-start.1
  95.5 11.4 %shard_map.75 = f32[512,512]{1,0:T(8,128)S(1)} custom-call(f32[27]{0:T(128)S(1)} %reshape.29.coeffs_ref, f32[2]{0:T(128)S(1)} %pad_maximum_fusion.3.origin_ref, bf16[544,640]{1,0:T(8,128)(2,1)S(1)} %fusion.9.padded_ref, f32[16,256]{1,0:T(8,128)S(1)} %get-tuple-element.14.rows_ref, f32[16,256]{1,0:T(8,128)S(1)} %get-tuple-element.13.cols_ref), custom_call_target="tpu_custom_call" | custom-call | flops 3000000000 | bytes 2000000 | tf_op jit(solution)/shard_map/pallas_call | solution.py:91
  107.0 0.0 copy-done.1
  107.0 0.3 convert_reduce_fusion
  107.3 2.0 %all-to-all-done.1 = bf16[128,16,128]{2,1,0:T(8,128)(2,1)S(1)} async-done(((bf16[128,16,128]{2,1,0:T(8,128)(2,1)}), bf16[128,16,128]{2,1,0:T(8,128)(2,1)S(1)}, u32[]{:S(2)}, u32[]{:S(2)}) %all-to-all-start.1) | async-done | bytes 524320 | tf_op jit(solution)/shard_map/all_to_all | solution.py:236
  109.3 0.1 convert_multiply_fusion
  109.4 0.2 copy.12
  109.6 1.0 fusion.6
  (3 shorter events, 0.0 us)
Async XLA Ops:
  5.4 11.9 %copy-start = (bf16[512,512]{1,0:T(8,128)(2,1)S(1)}, bf16[512,512]{1,0:T(8,128)(2,1)}, u32[]{:S(2)}) copy-start(bf16[512,512]{1,0:T(8,128)(2,1)} %param.10) | copy-start | bytes 1572868
  5.5 17.5 %copy-start.2 = (bf16[9,31]{1,0:T(8,128)(2,1)S(1)}, bf16[9,31]{1,0:T(8,128)(2,1)}, u32[]{:S(2)}) copy-start(bf16[9,31]{1,0:T(8,128)(2,1)} %param.12) | copy-start | bytes 1678
  5.5 17.5 %copy-start.3 = (bf16[9,31]{1,0:T(8,128)(2,1)S(1)}, bf16[9,31]{1,0:T(8,128)(2,1)}, u32[]{:S(2)}) copy-start(bf16[9,31]{1,0:T(8,128)(2,1)} %param.11) | copy-start | bytes 1678
  5.5 71.0 %all-to-all-start = ((bf16[128,136,128]{2,1,0:T(8,128)(2,1)}), bf16[128,136,128]{2,1,0:T(8,128)(2,1)}, u32[]{:S(2)}, u32[]{:S(2)}) async-start(bf16[128,136,128]{2,1,0:T(8,128)(2,1)} %shard_map.73), calls=%async_computation | async-start | bytes 8912896 | tf_op jit(solution)/shard_map/all_to_all | solution.py:233
  17.4 55.4 %copy-start.4 = (f32[9,3]{0,1:T(4,128)S(1)}, f32[9,3]{0,1:T(4,128)}, u32[]{:S(2)}) copy-start(f32[9,3]{0,1:T(4,128)} %param.13) | copy-start | bytes 328
  17.5 48.5 %collective-permute-start = (bf16[512,15]{1,0:T(8,128)(2,1)S(1)}, bf16[512,15]{1,0:T(8,128)(2,1)S(1)}, u32[]{:S(2)}, u32[]{:S(2)}) collective-permute-start(bf16[512,15]{1,0:T(8,128)(2,1)S(1)} %get-tuple-element.11), channel_id=1, source_target_pairs={{0,4},{4,8},{8,12},{12,16},{16,20},{20,24},{24,28},{28,32},{32,36}... | collective-permute-start | bytes 46088 | tf_op jit(solution)/shard_map/ppermute | solution.py:29
  21.1 47.1 %collective-permute-start.1 = (bf16[512,15]{1,0:T(8,128)(2,1)S(1)}, bf16[512,15]{1,0:T(8,128)(2,1)S(1)}, u32[]{:S(2)}, u32[]{:S(2)}) collective-permute-start(bf16[512,15]{1,0:T(8,128)(2,1)S(1)} %get-tuple-element.12), channel_id=1, source_target_pairs={{4,0},{8,4},{12,8},{16,12},{20,16},{24,20},{28,24},{32,28},{36,32}... | collective-permute-start | bytes 46088 | tf_op jit(solution)/shard_map/ppermute | solution.py:29
  68.3 4.7 %collective-permute-start.2 = (bf16[15,542]{1,0:T(8,128)(2,1)S(1)}, bf16[15,542]{1,0:T(8,128)(2,1)S(1)}, u32[]{:S(2)}, u32[]{:S(2)}) collective-permute-start(bf16[15,542]{1,0:T(8,128)(2,1)S(1)} %get-tuple-element.9), channel_id=1, source_target_pairs={{0,1},{1,2},{2,3},{4,5},{5,6},{6,7},{8,9},{9,10},{10,11},{12,13},{... | collective-permute-start | bytes 48788 | tf_op jit(solution)/shard_map/ppermute | solution.py:29
  71.4 4.5 %collective-permute-start.3 = (bf16[15,542]{1,0:T(8,128)(2,1)S(1)}, bf16[15,542]{1,0:T(8,128)(2,1)S(1)}, u32[]{:S(2)}, u32[]{:S(2)}) collective-permute-start(bf16[15,542]{1,0:T(8,128)(2,1)S(1)} %get-tuple-element.10), channel_id=1, source_target_pairs={{1,0},{2,1},{3,2},{5,4},{6,5},{7,6},{9,8},{10,9},{11,10},{13,12},{... | collective-permute-start | bytes 48788 | tf_op jit(solution)/shard_map/ppermute | solution.py:29
  85.7 23.6 %all-to-all-start.1 = ((bf16[128,16,128]{2,1,0:T(8,128)(2,1)}), bf16[128,16,128]{2,1,0:T(8,128)(2,1)S(1)}, u32[]{:S(2)}, u32[]{:S(2)}) async-start(bf16[128,16,128]{2,1,0:T(8,128)(2,1)} %get-tuple-element.7), calls=%async_computation.1 | async-start | bytes 1048576 | tf_op jit(solution)/shard_map/all_to_all | solution.py:236
  95.5 11.4 %copy-start.1 = (f32[128,128]{1,0:T(8,128)S(1)}, f32[128,128]{1,0:T(8,128)}, u32[]{:S(2)}) copy-start(f32[128,128]{1,0:T(8,128)} %get-tuple-element.8) | copy-start | bytes 196612

commit v3 on v2

--- a/solution.py
+++ b/solution.py
@@ -29,14 +29,14 @@
     return lax.ppermute(cells, axis, pairs)
 
 
-def with_halo(template):
+def with_halo(template, blank):
     left = edge_shift(template[:, EXTENT - HALF:], "col", True)
     right = edge_shift(template[:, :HALF], "col", False)
     wide = jnp.concatenate([left, template, right], axis=1)
     above = edge_shift(wide[EXTENT - HALF:], "row", True)
     below = edge_shift(wide[:HALF], "row", False)
     tall = jnp.concatenate([above, wide, below], axis=0)
-    return jnp.pad(tall, ((0, 2), (0, 98)))
+    return (jnp.pad(tall, ((0, 2), (0, 98))).astype(jnp.float32) + blank).astype(jnp.bfloat16)
 
 
 def toeplitz(taps_row):
@@ -46,37 +46,32 @@
 
 def model_kernel(coeffs_ref, origin_ref, padded_ref, rows_ref, cols_ref, model_ref, band_rows, band_cols, passed):
     for b in range(BASES):
-        band_rows[b] = toeplitz(rows_ref[b:b + 1, :])
+        band_rows[b * TB:(b + 1) * TB, :] = toeplitz(rows_ref[b:b + 1, :])
         band_cols[b] = toeplitz(cols_ref[b:b + 1, :])
     height_all = float(EXTENT * 4)
     width_all = float(EXTENT * 32)
-
-    @pl.loop(0, GRID)
-    def _(q):
-        source = padded_ref[pl.ds(pl.multiple_of(q * TB, TB), 160), :]
-
-        @pl.loop(0, BASES)
-        def _(b):
-            passed[b] = jnp.dot(
-                band_rows[b][:, :160], source, preferred_element_type=jnp.float32
-            ).astype(jnp.bfloat16)
-
-        local_y = lax.broadcasted_iota(jnp.int32, (TB, TB), 0) + q * TB
-        coord_y = 2.0 * (local_y.astype(jnp.float32) + (origin_ref[0] + 0.5)) / height_all - 1.0
-        for p in range(GRID):
-            local_x = lax.broadcasted_iota(jnp.int32, (TB, TB), 1) + p * TB
-            coord_x = 2.0 * (local_x.astype(jnp.float32) + (origin_ref[1] + 0.5)) / width_all - 1.0
-            total = jnp.zeros((TB, TB), jnp.float32)
-            for b in range(BASES):
-                image = lax.dot_general(
-                    passed[b, :, p * TB:(p + 2) * TB],
-                    band_cols[b],
-                    (((1,), (1,)), ((), ())),
-                    preferred_element_type=jnp.float32,
-                )
-                weight = coeffs_ref[3 * b] + coeffs_ref[3 * b + 1] * coord_x + coeffs_ref[3 * b + 2] * coord_y
-                total = total + weight * image
-            model_ref[pl.ds(pl.multiple_of(q * TB, TB), TB), p * TB:(p + 1) * TB] = total
+    for q in range(GRID):
+        stacked = jnp.dot(
+            band_rows[:, :160], padded_ref[q * TB:q * TB + 160, :], preferred_element_type=jnp.float32
+        ).astype(jnp.bfloat16)
+        for b in range(BASES):
+            passed[b, q * TB:(q + 1) * TB, :] = stacked[b * TB:(b + 1) * TB, :]
+    local_y = lax.broadcasted_iota(jnp.int32, (EXTENT, TB), 0)
+    coord_y = 2.0 * (local_y.astype(jnp.float32) + (origin_ref[0] + 0.5)) / height_all - 1.0
+    for p in range(GRID):
+        local_x = lax.broadcasted_iota(jnp.int32, (1, TB), 1) + p * TB
+        coord_x = 2.0 * (local_x.astype(jnp.float32) + (origin_ref[1] + 0.5)) / width_all - 1.0
+        total = jnp.zeros((EXTENT, TB), jnp.float32)
+        for b in range(BASES):
+            image = lax.dot_general(
+                passed[b, :, p * TB:(p + 2) * TB],
+                band_cols[b],
+                (((1,), (1,)), ((), ())),
+                preferred_element_type=jnp.float32,
+            )
+            weight = (coeffs_ref[3 * b] + coeffs_ref[3 * b + 1] * coord_x) + coeffs_ref[3 * b + 2] * coord_y
+            total = total + weight * image
+        model_ref[:, p * TB:(p + 1) * TB] = total
 
 
 def model_of(padded, kern_rows, kern_cols, coeffs):
@@ -94,11 +89,11 @@
         in_specs=[smem, smem, vmem, vmem, vmem],
         out_specs=vmem,
         scratch_shapes=[
+            pltpu.VMEM((BASES * TB, 2 * TB), jnp.bfloat16),
             pltpu.VMEM((BASES, TB, 2 * TB), jnp.bfloat16),
-            pltpu.VMEM((BASES, TB, 2 * TB), jnp.bfloat16),
-            pltpu.VMEM((BASES, TB, 640), jnp.bfloat16),
+            pltpu.VMEM((BASES, EXTENT, 640), jnp.bfloat16),
         ],
-        compiler_params=pltpu.CompilerParams(vmem_limit_bytes=24 << 20),
+        compiler_params=pltpu.CompilerParams(vmem_limit_bytes=32 << 20),
         cost_estimate=pl.CostEstimate(flops=3_000_000_000, bytes_accessed=2_000_000, transcendentals=0),
     )(coeffs.reshape(-1), origin, padded, taps_rows, taps_cols)
 
@@ -158,7 +153,7 @@
     )(dest.reshape(1, TB), slot.reshape(1, TB), blocks)
 
 
-def merge_kernel(arrived_ref, out_ref, keys_ref, labels, rows, acc, spread, labels_sem, rows_sem):
+def merge_kernel(arrived_ref, out_ref, keys_ref, blank_ref, labels, rows, acc, spread, labels_sem, rows_sem):
     named = pltpu.make_async_copy(arrived_ref.at[:, pl.ds(TB, 8), :], labels, labels_sem)
     named.start()
     arrivals = []
@@ -173,6 +168,7 @@
     tags = labels[...].astype(jnp.float32)
     keys = tags[:, 0, :] * 16.0 + tags[:, 1, :]
     keys_ref[...] = keys
+    blank_ref[...] = jnp.zeros_like(blank_ref)
     skewed = pltpu.roll(keys, 0, 1, stride=CHUNK, stride_axis=0)
     for k in range(PARTS):
         arrivals[k].wait()
@@ -212,9 +208,10 @@
         out_shape=(
             jax.ShapeDtypeStruct((TB, 16, TB), jnp.bfloat16),
             jax.ShapeDtypeStruct((TB, TB), jnp.float32),
+            jax.ShapeDtypeStruct((1, 640), jnp.float32),
         ),
         in_specs=[pl.BlockSpec(memory_space=pl.ANY)],
-        out_specs=(near, near),
+        out_specs=(near, near, near),
         scratch_shapes=[
             pltpu.VMEM((TB, 8, TB), jnp.bfloat16),
             pltpu.VMEM((PARTS, TB, CHUNK, TB), jnp.bfloat16),
@@ -231,8 +228,8 @@
 def body(blocks, dest, slot, template, kern_rows, kern_cols, coeffs):
     parcels = turned(blocks, dest, slot)
     arrived = lax.all_to_all(parcels, AXES, split_axis=0, concat_axis=0, tiled=True)
-    model = model_of(with_halo(template), kern_rows, kern_cols, coeffs)
-    sums, keys = merged(arrived)
+    sums, keys, blank = merged(arrived)
+    model = model_of(with_halo(template, blank), kern_rows, kern_cols, coeffs)
     gathered = lax.all_to_all(sums, AXES, split_axis=0, concat_axis=0, tiled=True)
     mine = lax.axis_index("col") * 4 + lax.axis_index("row")
     tiles = (mine * 16 + jnp.arange(16, dtype=jnp.int32)).astype(jnp.float32)

time: 111 us -> 108 us (0.973)
  Pallas kernels: 26.1 us -> 19.8 us
  waiting for transfers between devices: 50.1 us -> 52.6 us
    pallas_call x1, Pallas kernels: 11.4 us -> 5.11 us  [model_of(): pl.pallas_call(model_kernel, out_shape=jax.ShapeDtypeStruct((EXTENT, EXTE...]
    all_to_all x1, waiting for transfers between devices: 1.98 us -> 6.99 us  [body(): lax.all_to_all(sums, AXES, split_axis=0, concat_axis=0, tiled=True)]
    ppermute x4, waiting for transfers between devices: 48.1 us -> 44.9 us  [edge_shift(): return lax.ppermute(cells, axis, pairs)]
  transfers between devices with their start and end apart: 6 -> 6, of which waited for: 4 -> 4; matrix products, arithmetic and copies ran while one was open for 1% -> 2% of each run, Pallas kernels for 10% -> 13%
where the time goes in v3:
time: 108 us
  waiting for transfers between devices  52.6 us (49%)
  starting transfers between devices  31.6 us (29%)
  Pallas kernels  19.8 us (18%)
  other arithmetic  2.88 us (3%)
    ppermute x4, waiting for transfers between devices, edge_shift(): return lax.ppermute(cells, axis, pairs)  44.9 us
    all_to_all x1, starting transfers between devices, body(): lax.all_to_all(parcels, AXES, split_axis=0, concat_axis=0, tiled=True)  11.9 us
    all_to_all x1, starting transfers between devices, body(): lax.all_to_all(sums, AXES, split_axis=0, concat_axis=0, tiled=True)  9.89 us
    ppermute x4, starting transfers between devices, edge_shift(): return lax.ppermute(cells, axis, pairs)  9.84 us
    pallas_call x1, Pallas kernels, merged(): pl.pallas_call(merge_kernel, out_shape=(jax.ShapeDtypeStruct((TB, 16, TB)...  9.23 us
    all_to_all x1, waiting for transfers between devices, body(): lax.all_to_all(sums, AXES, split_axis=0, concat_axis=0, tiled=True)  6.99 us
    pallas_call x1, Pallas kernels, turned(): pl.pallas_call(turn_kernel, out_shape=jax.ShapeDtypeStruct((TB, TB + 8, T...  5.45 us
    pallas_call x1, Pallas kernels, model_of(): pl.pallas_call(model_kernel, out_shape=jax.ShapeDtypeStruct((EXTENT, EXTE...  5.11 us
  transfers between devices with their start and end apart: 6, of which 4 were waited for; matrix products, arithmetic and copies ran while one was open for 2% of the time, Pallas kernels for 13%

profile of v3, /device:TPU:1, one launch (start us, length us, event | category | flops | bytes accessed | tf_op | source)
XLA Modules:
  0.0 107.6 jit_solution(2442586562165815555)
XLA Ops:
  0.0 5.4 %shard_map.73 = bf16[128,136,128]{2,1,0:T(8,128)(2,1)} custom-call(s32[1,128]{1,0:T(1,128)} %bitcast.14, s32[1,128]{1,0:T(1,128)} %bitcast.15, bf16[128,128,128]{2,1,0:T(8,128)(2,1)} %blocks_ref.1), custom_call_target="tpu_custom_call" | custom-call | flops 600000000 | bytes 8700000 | tf_op jit(solution)/shard_map/pallas_call | solution.py:139
  5.5 0.0 copy-start
  5.5 0.0 copy-start.2
  5.5 0.0 copy-start.3
  5.5 0.0 copy-start.4
  5.5 11.9 %all-to-all-start = ((bf16[128,136,128]{2,1,0:T(8,128)(2,1)}), bf16[128,136,128]{2,1,0:T(8,128)(2,1)}, u32[]{:S(2)}, u32[]{:S(2)}) async-start(bf16[128,136,128]{2,1,0:T(8,128)(2,1)} %shard_map.73), calls=%async_computation | async-start | bytes 8912896 | tf_op jit(solution)/shard_map/all_to_all | solution.py:230
  17.4 0.0 copy-done
  17.4 0.1 fusion.16
  17.5 3.5 %collective-permute-start = (bf16[512,15]{1,0:T(8,128)(2,1)S(1)}, bf16[512,15]{1,0:T(8,128)(2,1)S(1)}, u32[]{:S(2)}, u32[]{:S(2)}) collective-permute-start(bf16[512,15]{1,0:T(8,128)(2,1)S(1)} %get-tuple-element.13), channel_id=1, source_target_pairs={{0,4},{4,8},{8,12},{12,16},{16,20},{20,24},{24,28},{28,32},{32,36}... | collective-permute-start | bytes 46088 | tf_op jit(solution)/shard_map/ppermute | solution.py:29
  21.1 1.9 %collective-permute-start.1 = (bf16[512,15]{1,0:T(8,128)(2,1)S(1)}, bf16[512,15]{1,0:T(8,128)(2,1)S(1)}, u32[]{:S(2)}, u32[]{:S(2)}) collective-permute-start(bf16[512,15]{1,0:T(8,128)(2,1)S(1)} %get-tuple-element.14), channel_id=1, source_target_pairs={{4,0},{8,4},{12,8},{16,12},{20,16},{24,20},{28,24},{32,28},{36,32}... | collective-permute-start | bytes 46088 | tf_op jit(solution)/shard_map/ppermute | solution.py:29
  23.0 0.0 copy-done.2
  23.0 0.0 copy-done.3
  23.1 0.1 pad_maximum_fusion.3.origin_ref
  23.1 0.0 copy-done.4
  23.1 0.1 copy.13
  23.2 0.1 reshape.29.coeffs_ref
  23.3 42.7 %collective-permute-done = bf16[512,15]{1,0:T(8,128)(2,1)S(1)} collective-permute-done((bf16[512,15]{1,0:T(8,128)(2,1)S(1)}, bf16[512,15]{1,0:T(8,128)(2,1)S(1)}, u32[]{:S(2)}, u32[]{:S(2)}) %collective-permute-start) | collective-permute-done | bytes 15392 | tf_op jit(solution)/shard_map/ppermute | solution.py:29
  66.0 2.2 %collective-permute-done.1 = bf16[512,15]{1,0:T(8,128)(2,1)S(1)} collective-permute-done((bf16[512,15]{1,0:T(8,128)(2,1)S(1)}, bf16[512,15]{1,0:T(8,128)(2,1)S(1)}, u32[]{:S(2)}, u32[]{:S(2)}) %collective-permute-start.1) | collective-permute-done | bytes 15392 | tf_op jit(solution)/shard_map/ppermute | solution.py:29
  68.2 0.1 pad_maximum_fusion.2
  68.3 3.1 %collective-permute-start.2 = (bf16[15,542]{1,0:T(8,128)(2,1)S(1)}, bf16[15,542]{1,0:T(8,128)(2,1)S(1)}, u32[]{:S(2)}, u32[]{:S(2)}) collective-permute-start(bf16[15,542]{1,0:T(8,128)(2,1)S(1)} %get-tuple-element.11), channel_id=1, source_target_pairs={{0,1},{1,2},{2,3},{4,5},{5,6},{6,7},{8,9},{9,10},{10,11},{12,13},{... | collective-permute-start | bytes 48788 | tf_op jit(solution)/shard_map/ppermute | solution.py:29
  71.4 1.3 %collective-permute-start.3 = (bf16[15,542]{1,0:T(8,128)(2,1)S(1)}, bf16[15,542]{1,0:T(8,128)(2,1)S(1)}, u32[]{:S(2)}, u32[]{:S(2)}) collective-permute-start(bf16[15,542]{1,0:T(8,128)(2,1)S(1)} %get-tuple-element.12), channel_id=1, source_target_pairs={{1,0},{2,1},{3,2},{5,4},{6,5},{7,6},{9,8},{10,9},{11,10},{13,12},{... | collective-permute-start | bytes 48788 | tf_op jit(solution)/shard_map/ppermute | solution.py:29
  72.7 0.7 all-to-all-done.arrived_ref
  73.4 9.2 %shard_map.74 = (bf16[128,16,128]{2,1,0:T(8,128)(2,1)}, f32[128,128]{1,0:T(8,128)}, f32[1,640]{1,0:T(1,128)}) custom-call(bf16[128,136,128]{2,1,0:T(8,128)(2,1)} %all-to-all-done.arrived_ref), custom_call_target="tpu_custom_call" | custom-call | flops 5000000000 | bytes 5000000 | tf_op jit(solution)/shard_map/pallas_call | solution.py:206
  82.7 0.0 copy-start.1
  82.7 9.9 %all-to-all-start.1 = ((bf16[128,16,128]{2,1,0:T(8,128)(2,1)}), bf16[128,16,128]{2,1,0:T(8,128)(2,1)S(1)}, u32[]{:S(2)}, u32[]{:S(2)}) async-start(bf16[128,16,128]{2,1,0:T(8,128)(2,1)} %get-tuple-element.8), calls=%async_computation.1 | async-start | bytes 1048576 | tf_op jit(solution)/shard_map/all_to_all | solution.py:233
  92.6 0.7 reduce
  93.3 0.0 collective-permute-done.2
  93.3 0.0 collective-permute-done.3
  93.3 0.6 add_convert_fusion.padded_ref
  93.9 0.0 copy-done.1
  93.9 0.3 convert_reduce_fusion
  94.2 5.1 %shard_map.75 = f32[512,512]{1,0:T(8,128)S(1)} custom-call(f32[27]{0:T(128)S(1)} %reshape.29.coeffs_ref, f32[2]{0:T(128)S(1)} %pad_maximum_fusion.3.origin_ref, bf16[544,640]{1,0:T(8,128)(2,1)S(1)} %add_convert_fusion.padded_ref, f32[16,256]{1,0:T(8,128)S(1)} %get-tuple-element.16.rows_ref, f32[16,256]{1,0:T(8,128)S(1)} %get-tuple-element.15.cols_ref), custom_call_target="tpu_custom_call" | custom-call | flops 3000000000 | bytes 2000000 | tf_op jit(solution)/shard_map/pallas_call | solution.py:86
  99.3 7.0 %all-to-all-done.1 = bf16[128,16,128]{2,1,0:T(8,128)(2,1)S(1)} async-done(((bf16[128,16,128]{2,1,0:T(8,128)(2,1)}), bf16[128,16,128]{2,1,0:T(8,128)(2,1)S(1)}, u32[]{:S(2)}, u32[]{:S(2)}) %all-to-all-start.1) | async-done | bytes 524320 | tf_op jit(solution)/shard_map/all_to_all | solution.py:233
  106.3 0.1 convert_multiply_fusion
  106.5 0.2 copy.12
  106.7 1.0 fusion.6
  (3 shorter events, 0.0 us)
Async XLA Ops:
  5.5 12.0 %copy-start = (bf16[512,512]{1,0:T(8,128)(2,1)S(1)}, bf16[512,512]{1,0:T(8,128)(2,1)}, u32[]{:S(2)}) copy-start(bf16[512,512]{1,0:T(8,128)(2,1)} %param.10) | copy-start | bytes 1572868
  5.5 17.6 %copy-start.2 = (bf16[9,31]{1,0:T(8,128)(2,1)S(1)}, bf16[9,31]{1,0:T(8,128)(2,1)}, u32[]{:S(2)}) copy-start(bf16[9,31]{1,0:T(8,128)(2,1)} %param.12) | copy-start | bytes 1678
  5.5 17.6 %copy-start.3 = (bf16[9,31]{1,0:T(8,128)(2,1)S(1)}, bf16[9,31]{1,0:T(8,128)(2,1)}, u32[]{:S(2)}) copy-start(bf16[9,31]{1,0:T(8,128)(2,1)} %param.11) | copy-start | bytes 1678
  5.5 17.7 %copy-start.4 = (f32[9,3]{0,1:T(4,128)S(1)}, f32[9,3]{0,1:T(4,128)}, u32[]{:S(2)}) copy-start(f32[9,3]{0,1:T(4,128)} %param.13) | copy-start | bytes 328
  5.5 67.9 %all-to-all-start = ((bf16[128,136,128]{2,1,0:T(8,128)(2,1)}), bf16[128,136,128]{2,1,0:T(8,128)(2,1)}, u32[]{:S(2)}, u32[]{:S(2)}) async-start(bf16[128,136,128]{2,1,0:T(8,128)(2,1)} %shard_map.73), calls=%async_computation | async-start | bytes 8912896 | tf_op jit(solution)/shard_map/all_to_all | solution.py:230
  17.5 48.5 %collective-permute-start = (bf16[512,15]{1,0:T(8,128)(2,1)S(1)}, bf16[512,15]{1,0:T(8,128)(2,1)S(1)}, u32[]{:S(2)}, u32[]{:S(2)}) collective-permute-start(bf16[512,15]{1,0:T(8,128)(2,1)S(1)} %get-tuple-element.13), channel_id=1, source_target_pairs={{0,4},{4,8},{8,12},{12,16},{16,20},{20,24},{24,28},{28,32},{32,36}... | collective-permute-start | bytes 46088 | tf_op jit(solution)/shard_map/ppermute | solution.py:29
  21.1 47.2 %collective-permute-start.1 = (bf16[512,15]{1,0:T(8,128)(2,1)S(1)}, bf16[512,15]{1,0:T(8,128)(2,1)S(1)}, u32[]{:S(2)}, u32[]{:S(2)}) collective-permute-start(bf16[512,15]{1,0:T(8,128)(2,1)S(1)} %get-tuple-element.14), channel_id=1, source_target_pairs={{4,0},{8,4},{12,8},{16,12},{20,16},{24,20},{28,24},{32,28},{36,32}... | collective-permute-start | bytes 46088 | tf_op jit(solution)/shard_map/ppermute | solution.py:29
  68.3 24.9 %collective-permute-start.2 = (bf16[15,542]{1,0:T(8,128)(2,1)S(1)}, bf16[15,542]{1,0:T(8,128)(2,1)S(1)}, u32[]{:S(2)}, u32[]{:S(2)}) collective-permute-start(bf16[15,542]{1,0:T(8,128)(2,1)S(1)} %get-tuple-element.11), channel_id=1, source_target_pairs={{0,1},{1,2},{2,3},{4,5},{5,6},{6,7},{8,9},{9,10},{10,11},{12,13},{... | collective-permute-start | bytes 48788 | tf_op jit(solution)/shard_map/ppermute | solution.py:29
  71.4 21.8 %collective-permute-start.3 = (bf16[15,542]{1,0:T(8,128)(2,1)S(1)}, bf16[15,542]{1,0:T(8,128)(2,1)S(1)}, u32[]{:S(2)}, u32[]{:S(2)}) collective-permute-start(bf16[15,542]{1,0:T(8,128)(2,1)S(1)} %get-tuple-element.12), channel_id=1, source_target_pairs={{1,0},{2,1},{3,2},{5,4},{6,5},{7,6},{9,8},{10,9},{11,10},{13,12},{... | collective-permute-start | bytes 48788 | tf_op jit(solution)/shard_map/ppermute | solution.py:29
  82.7 11.2 %copy-start.1 = (f32[128,128]{1,0:T(8,128)S(1)}, f32[128,128]{1,0:T(8,128)}, u32[]{:S(2)}) copy-start(f32[128,128]{1,0:T(8,128)} %get-tuple-element.9) | copy-start | bytes 196612
  82.7 23.6 %all-to-all-start.1 = ((bf16[128,16,128]{2,1,0:T(8,128)(2,1)}), bf16[128,16,128]{2,1,0:T(8,128)(2,1)S(1)}, u32[]{:S(2)}, u32[]{:S(2)}) async-start(bf16[128,16,128]{2,1,0:T(8,128)(2,1)} %get-tuple-element.8), calls=%async_computation.1 | async-start | bytes 1048576 | tf_op jit(solution)/shard_map/all_to_all | solution.py:233

commit v4 on v3

--- a/solution.py
+++ b/solution.py
@@ -184,10 +184,10 @@
             taken = rows[k, g * 8:(g + 1) * 8].reshape(TB, TB)
             mask = jnp.broadcast_to(high_down[:, g:g + 1], (TB, TB)).astype(jnp.bfloat16)
             upper = taken * mask
-            spread[k % 2, g * TB:(g + 1) * TB, TB:] = upper
-            spread[k % 2, g * TB:(g + 1) * TB, :TB] = taken - upper
+            spread[k % 4, g * TB:(g + 1) * TB, TB:] = upper
+            spread[k % 4, g * TB:(g + 1) * TB, :TB] = taken - upper
         line = jnp.concatenate([places[g:g + 1, :] for g in range(16)], axis=1)
-        for first, size in ((0, 256), (256, 320)):
+        for first, size in ((0, 320), (320, 256)):
             middle = size // 2
             marks = (lax.broadcasted_iota(jnp.int32, (size, DEPTH), 0) - middle).astype(jnp.bfloat16)
             wanted = (line - float(first + middle)).astype(jnp.bfloat16)
@@ -195,7 +195,7 @@
             total = acc[window, :]
             for q in range(0, 16 * TB, DEPTH):
                 chosen = jnp.where(marks == wanted[:, q:q + DEPTH], jnp.bfloat16(1), jnp.bfloat16(0))
-                total = total + jnp.dot(chosen, spread[k % 2, q:q + DEPTH, :], preferred_element_type=jnp.float32)
+                total = total + jnp.dot(chosen, spread[k % 4, q:q + DEPTH, :], preferred_element_type=jnp.float32)
             acc[window, :] = total
     whole = acc[...].reshape(TB, 8, 2 * TB)
     out_ref[...] = jnp.concatenate([whole[:, :, :TB], whole[:, :, TB:]], axis=1).astype(jnp.bfloat16)
@@ -216,7 +216,7 @@
             pltpu.VMEM((TB, 8, TB), jnp.bfloat16),
             pltpu.VMEM((PARTS, TB, CHUNK, TB), jnp.bfloat16),
             pltpu.VMEM((1024, 2 * TB), jnp.float32),
-            pltpu.VMEM((2, 16 * TB, 2 * TB), jnp.bfloat16),
+            pltpu.VMEM((4, 16 * TB, 2 * TB), jnp.bfloat16),
             pltpu.SemaphoreType.DMA,
             pltpu.SemaphoreType.DMA((PARTS,)),
         ],

time: 108 us -> 108 us (level)
  no operation moved by 1% of the time
where the time goes in v4:
time: 108 us; the launch traced here: 107 us
  waiting for transfers between devices  52.7 us (49%)
  starting transfers between devices  31.6 us (29%)
  Pallas kernels  19.6 us (18%)
  other arithmetic  2.88 us (3%)
    ppermute x4, waiting for transfers between devices, edge_shift(): return lax.ppermute(cells, axis, pairs)  44.9 us
    all_to_all x1, starting transfers between devices, body(): lax.all_to_all(parcels, AXES, split_axis=0, concat_axis=0, tiled=True)  11.9 us
    all_to_all x1, starting transfers between devices, body(): lax.all_to_all(sums, AXES, split_axis=0, concat_axis=0, tiled=True)  9.9 us
    ppermute x4, starting transfers between devices, edge_shift(): return lax.ppermute(cells, axis, pairs)  9.84 us
    pallas_call x1, Pallas kernels, merged(): pl.pallas_call(merge_kernel, out_shape=(jax.ShapeDtypeStruct((TB, 16, TB)...  9.05 us
    all_to_all x1, waiting for transfers between devices, body(): lax.all_to_all(sums, AXES, split_axis=0, concat_axis=0, tiled=True)  7.03 us
    pallas_call x1, Pallas kernels, turned(): pl.pallas_call(turn_kernel, out_shape=jax.ShapeDtypeStruct((TB, TB + 8, T...  5.45 us
    pallas_call x1, Pallas kernels, model_of(): pl.pallas_call(model_kernel, out_shape=jax.ShapeDtypeStruct((EXTENT, EXTE...  5.07 us
  transfers between devices with their start and end apart: 6, of which 4 were waited for; matrix products, arithmetic and copies ran while one was open for 2% of the time, Pallas kernels for 13%

profile of v4, /device:TPU:1, one launch (start us, length us, event | category | flops | bytes accessed | tf_op | source)
XLA Modules:
  0.0 107.5 jit_solution(4791556664178520069)
XLA Ops:
  0.0 5.4 %shard_map.73 = bf16[128,136,128]{2,1,0:T(8,128)(2,1)} custom-call(s32[1,128]{1,0:T(1,128)} %bitcast.14, s32[1,128]{1,0:T(1,128)} %bitcast.15, bf16[128,128,128]{2,1,0:T(8,128)(2,1)} %blocks_ref.1), custom_call_target="tpu_custom_call" | custom-call | flops 600000000 | bytes 8700000 | tf_op jit(solution)/shard_map/pallas_call | solution.py:139
  5.5 0.0 copy-start
  5.5 0.0 copy-start.2
  5.5 0.0 copy-start.3
  5.5 0.0 copy-start.4
  5.5 11.9 %all-to-all-start = ((bf16[128,136,128]{2,1,0:T(8,128)(2,1)}), bf16[128,136,128]{2,1,0:T(8,128)(2,1)}, u32[]{:S(2)}, u32[]{:S(2)}) async-start(bf16[128,136,128]{2,1,0:T(8,128)(2,1)} %shard_map.73), calls=%async_computation | async-start | bytes 8912896 | tf_op jit(solution)/shard_map/all_to_all | solution.py:230
  17.4 0.0 copy-done
  17.4 0.1 fusion.16
  17.5 3.5 %collective-permute-start = (bf16[512,15]{1,0:T(8,128)(2,1)S(1)}, bf16[512,15]{1,0:T(8,128)(2,1)S(1)}, u32[]{:S(2)}, u32[]{:S(2)}) collective-permute-start(bf16[512,15]{1,0:T(8,128)(2,1)S(1)} %get-tuple-element.13), channel_id=1, source_target_pairs={{0,4},{4,8},{8,12},{12,16},{16,20},{20,24},{24,28},{28,32},{32,36}... | collective-permute-start | bytes 46088 | tf_op jit(solution)/shard_map/ppermute | solution.py:29
  21.1 1.9 %collective-permute-start.1 = (bf16[512,15]{1,0:T(8,128)(2,1)S(1)}, bf16[512,15]{1,0:T(8,128)(2,1)S(1)}, u32[]{:S(2)}, u32[]{:S(2)}) collective-permute-start(bf16[512,15]{1,0:T(8,128)(2,1)S(1)} %get-tuple-element.14), channel_id=1, source_target_pairs={{4,0},{8,4},{12,8},{16,12},{20,16},{24,20},{28,24},{32,28},{36,32}... | collective-permute-start | bytes 46088 | tf_op jit(solution)/shard_map/ppermute | solution.py:29
  23.0 0.0 copy-done.2
  23.0 0.0 copy-done.3
  23.1 0.1 pad_maximum_fusion.3.origin_ref
  23.1 0.0 copy-done.4
  23.1 0.1 copy.13
  23.2 0.1 reshape.29.coeffs_ref
  23.3 42.7 %collective-permute-done = bf16[512,15]{1,0:T(8,128)(2,1)S(1)} collective-permute-done((bf16[512,15]{1,0:T(8,128)(2,1)S(1)}, bf16[512,15]{1,0:T(8,128)(2,1)S(1)}, u32[]{:S(2)}, u32[]{:S(2)}) %collective-permute-start) | collective-permute-done | bytes 15392 | tf_op jit(solution)/shard_map/ppermute | solution.py:29
  66.0 2.2 %collective-permute-done.1 = bf16[512,15]{1,0:T(8,128)(2,1)S(1)} collective-permute-done((bf16[512,15]{1,0:T(8,128)(2,1)S(1)}, bf16[512,15]{1,0:T(8,128)(2,1)S(1)}, u32[]{:S(2)}, u32[]{:S(2)}) %collective-permute-start.1) | collective-permute-done | bytes 15392 | tf_op jit(solution)/shard_map/ppermute | solution.py:29
  68.2 0.1 pad_maximum_fusion.2
  68.3 3.1 %collective-permute-start.2 = (bf16[15,542]{1,0:T(8,128)(2,1)S(1)}, bf16[15,542]{1,0:T(8,128)(2,1)S(1)}, u32[]{:S(2)}, u32[]{:S(2)}) collective-permute-start(bf16[15,542]{1,0:T(8,128)(2,1)S(1)} %get-tuple-element.11), channel_id=1, source_target_pairs={{0,1},{1,2},{2,3},{4,5},{5,6},{6,7},{8,9},{9,10},{10,11},{12,13},{... | collective-permute-start | bytes 48788 | tf_op jit(solution)/shard_map/ppermute | solution.py:29
  71.4 1.3 %collective-permute-start.3 = (bf16[15,542]{1,0:T(8,128)(2,1)S(1)}, bf16[15,542]{1,0:T(8,128)(2,1)S(1)}, u32[]{:S(2)}, u32[]{:S(2)}) collective-permute-start(bf16[15,542]{1,0:T(8,128)(2,1)S(1)} %get-tuple-element.12), channel_id=1, source_target_pairs={{1,0},{2,1},{3,2},{5,4},{6,5},{7,6},{9,8},{10,9},{11,10},{13,12},{... | collective-permute-start | bytes 48788 | tf_op jit(solution)/shard_map/ppermute | solution.py:29
  72.7 0.7 all-to-all-done.arrived_ref
  73.4 9.1 %shard_map.74 = (bf16[128,16,128]{2,1,0:T(8,128)(2,1)}, f32[128,128]{1,0:T(8,128)}, f32[1,640]{1,0:T(1,128)}) custom-call(bf16[128,136,128]{2,1,0:T(8,128)(2,1)} %all-to-all-done.arrived_ref), custom_call_target="tpu_custom_call" | custom-call | flops 5000000000 | bytes 5000000 | tf_op jit(solution)/shard_map/pallas_call | solution.py:206
  82.5 0.0 copy-start.1
  82.5 9.9 %all-to-all-start.1 = ((bf16[128,16,128]{2,1,0:T(8,128)(2,1)}), bf16[128,16,128]{2,1,0:T(8,128)(2,1)S(1)}, u32[]{:S(2)}, u32[]{:S(2)}) async-start(bf16[128,16,128]{2,1,0:T(8,128)(2,1)} %get-tuple-element.8), calls=%async_computation.1 | async-start | bytes 1048576 | tf_op jit(solution)/shard_map/all_to_all | solution.py:233
  92.4 0.7 reduce
  93.1 0.0 collective-permute-done.2
  93.1 0.0 collective-permute-done.3
  93.1 0.6 add_convert_fusion.padded_ref
  93.7 0.0 copy-done.1
  93.7 0.3 convert_reduce_fusion
  94.1 5.1 %shard_map.75 = f32[512,512]{1,0:T(8,128)S(1)} custom-call(f32[27]{0:T(128)S(1)} %reshape.29.coeffs_ref, f32[2]{0:T(128)S(1)} %pad_maximum_fusion.3.origin_ref, bf16[544,640]{1,0:T(8,128)(2,1)S(1)} %add_convert_fusion.padded_ref, f32[16,256]{1,0:T(8,128)S(1)} %get-tuple-element.16.rows_ref, f32[16,256]{1,0:T(8,128)S(1)} %get-tuple-element.15.cols_ref), custom_call_target="tpu_custom_call" | custom-call | flops 3000000000 | bytes 2000000 | tf_op jit(solution)/shard_map/pallas_call | solution.py:86
  99.1 7.0 %all-to-all-done.1 = bf16[128,16,128]{2,1,0:T(8,128)(2,1)S(1)} async-done(((bf16[128,16,128]{2,1,0:T(8,128)(2,1)}), bf16[128,16,128]{2,1,0:T(8,128)(2,1)S(1)}, u32[]{:S(2)}, u32[]{:S(2)}) %all-to-all-start.1) | async-done | bytes 524320 | tf_op jit(solution)/shard_map/all_to_all | solution.py:233
  106.2 0.1 convert_multiply_fusion
  106.3 0.2 copy.12
  106.5 1.0 fusion.6
  (3 shorter events, 0.0 us)
Async XLA Ops:
  5.5 12.0 %copy-start = (bf16[512,512]{1,0:T(8,128)(2,1)S(1)}, bf16[512,512]{1,0:T(8,128)(2,1)}, u32[]{:S(2)}) copy-start(bf16[512,512]{1,0:T(8,128)(2,1)} %param.10) | copy-start | bytes 1572868
  5.5 17.6 %copy-start.2 = (bf16[9,31]{1,0:T(8,128)(2,1)S(1)}, bf16[9,31]{1,0:T(8,128)(2,1)}, u32[]{:S(2)}) copy-start(bf16[9,31]{1,0:T(8,128)(2,1)} %param.12) | copy-start | bytes 1678
  5.5 17.6 %copy-start.3 = (bf16[9,31]{1,0:T(8,128)(2,1)S(1)}, bf16[9,31]{1,0:T(8,128)(2,1)}, u32[]{:S(2)}) copy-start(bf16[9,31]{1,0:T(8,128)(2,1)} %param.11) | copy-start | bytes 1678
  5.5 17.7 %copy-start.4 = (f32[9,3]{0,1:T(4,128)S(1)}, f32[9,3]{0,1:T(4,128)}, u32[]{:S(2)}) copy-start(f32[9,3]{0,1:T(4,128)} %param.13) | copy-start | bytes 328
  5.5 67.9 %all-to-all-start = ((bf16[128,136,128]{2,1,0:T(8,128)(2,1)}), bf16[128,136,128]{2,1,0:T(8,128)(2,1)}, u32[]{:S(2)}, u32[]{:S(2)}) async-start(bf16[128,136,128]{2,1,0:T(8,128)(2,1)} %shard_map.73), calls=%async_computation | async-start | bytes 8912896 | tf_op jit(solution)/shard_map/all_to_all | solution.py:230
  17.5 48.5 %collective-permute-start = (bf16[512,15]{1,0:T(8,128)(2,1)S(1)}, bf16[512,15]{1,0:T(8,128)(2,1)S(1)}, u32[]{:S(2)}, u32[]{:S(2)}) collective-permute-start(bf16[512,15]{1,0:T(8,128)(2,1)S(1)} %get-tuple-element.13), channel_id=1, source_target_pairs={{0,4},{4,8},{8,12},{12,16},{16,20},{20,24},{24,28},{28,32},{32,36}... | collective-permute-start | bytes 46088 | tf_op jit(solution)/shard_map/ppermute | solution.py:29
  21.1 47.2 %collective-permute-start.1 = (bf16[512,15]{1,0:T(8,128)(2,1)S(1)}, bf16[512,15]{1,0:T(8,128)(2,1)S(1)}, u32[]{:S(2)}, u32[]{:S(2)}) collective-permute-start(bf16[512,15]{1,0:T(8,128)(2,1)S(1)} %get-tuple-element.14), channel_id=1, source_target_pairs={{4,0},{8,4},{12,8},{16,12},{20,16},{24,20},{28,24},{32,28},{36,32}... | collective-permute-start | bytes 46088 | tf_op jit(solution)/shard_map/ppermute | solution.py:29
  68.3 24.8 %collective-permute-start.2 = (bf16[15,542]{1,0:T(8,128)(2,1)S(1)}, bf16[15,542]{1,0:T(8,128)(2,1)S(1)}, u32[]{:S(2)}, u32[]{:S(2)}) collective-permute-start(bf16[15,542]{1,0:T(8,128)(2,1)S(1)} %get-tuple-element.11), channel_id=1, source_target_pairs={{0,1},{1,2},{2,3},{4,5},{5,6},{6,7},{8,9},{9,10},{10,11},{12,13},{... | collective-permute-start | bytes 48788 | tf_op jit(solution)/shard_map/ppermute | solution.py:29
  71.4 21.7 %collective-permute-start.3 = (bf16[15,542]{1,0:T(8,128)(2,1)S(1)}, bf16[15,542]{1,0:T(8,128)(2,1)S(1)}, u32[]{:S(2)}, u32[]{:S(2)}) collective-permute-start(bf16[15,542]{1,0:T(8,128)(2,1)S(1)} %get-tuple-element.12), channel_id=1, source_target_pairs={{1,0},{2,1},{3,2},{5,4},{6,5},{7,6},{9,8},{10,9},{11,10},{13,12},{... | collective-permute-start | bytes 48788 | tf_op jit(solution)/shard_map/ppermute | solution.py:29
  82.5 11.2 %copy-start.1 = (f32[128,128]{1,0:T(8,128)S(1)}, f32[128,128]{1,0:T(8,128)}, u32[]{:S(2)}) copy-start(f32[128,128]{1,0:T(8,128)} %get-tuple-element.9) | copy-start | bytes 196612
  82.5 23.7 %all-to-all-start.1 = ((bf16[128,16,128]{2,1,0:T(8,128)(2,1)}), bf16[128,16,128]{2,1,0:T(8,128)(2,1)S(1)}, u32[]{:S(2)}, u32[]{:S(2)}) async-start(bf16[128,16,128]{2,1,0:T(8,128)(2,1)} %get-tuple-element.8), calls=%async_computation.1 | async-start | bytes 1048576 | tf_op jit(solution)/shard_map/all_to_all | solution.py:233

commit v5 on v3

--- a/solution.py
+++ b/solution.py
@@ -30,12 +30,12 @@
 
 
 def with_halo(template, blank):
-    left = edge_shift(template[:, EXTENT - HALF:], "col", True)
-    right = edge_shift(template[:, :HALF], "col", False)
-    wide = jnp.concatenate([left, template, right], axis=1)
-    above = edge_shift(wide[EXTENT - HALF:], "row", True)
-    below = edge_shift(wide[:HALF], "row", False)
-    tall = jnp.concatenate([above, wide, below], axis=0)
+    above = edge_shift(template[EXTENT - HALF:], "row", True)
+    below = edge_shift(template[:HALF], "row", False)
+    tall = jnp.concatenate([above, template, below], axis=0)
+    left = edge_shift(tall[:, EXTENT - HALF:], "col", True)
+    right = edge_shift(tall[:, :HALF], "col", False)
+    tall = jnp.concatenate([left, tall, right], axis=1)
     return (jnp.pad(tall, ((0, 2), (0, 98))).astype(jnp.float32) + blank).astype(jnp.bfloat16)
 
 

time: 108 us -> 107 us (level)
  waiting for transfers between devices: 52.6 us -> 48.4 us
  starting transfers between devices: 31.6 us -> 35.2 us
    ppermute x4, starting transfers between devices: 9.84 us -> 14.4 us  [edge_shift(): return lax.ppermute(cells, axis, pairs)]
    ppermute x4, waiting for transfers between devices: 44.9 us -> 41.4 us  [edge_shift(): return lax.ppermute(cells, axis, pairs)]
    all_to_all x1, starting transfers between devices: 9.89 us -> 8.8 us  [body(): lax.all_to_all(sums, AXES, split_axis=0, concat_axis=0, tiled=True)]
  transfers between devices with their start and end apart: 6 -> 6, of which waited for: 4 -> 3; matrix products, arithmetic and copies ran while one was open for 2% -> 2% of each run, Pallas kernels for 13% -> 13%
where the time goes in v5:
time: 107 us
  waiting for transfers between devices  48.4 us (45%)
  starting transfers between devices  35.2 us (33%)
  Pallas kernels  19.8 us (19%)
  other arithmetic  2.89 us (3%)
    ppermute x4, waiting for transfers between devices, edge_shift(): return lax.ppermute(cells, axis, pairs)  41.4 us
    ppermute x4, starting transfers between devices, edge_shift(): return lax.ppermute(cells, axis, pairs)  14.4 us
    all_to_all x1, starting transfers between devices, body(): lax.all_to_all(parcels, AXES, split_axis=0, concat_axis=0, tiled=True)  11.9 us
    pallas_call x1, Pallas kernels, merged(): pl.pallas_call(merge_kernel, out_shape=(jax.ShapeDtypeStruct((TB, 16, TB)...  9.22 us
    all_to_all x1, starting transfers between devices, body(): lax.all_to_all(sums, AXES, split_axis=0, concat_axis=0, tiled=True)  8.8 us
    all_to_all x1, waiting for transfers between devices, body(): lax.all_to_all(sums, AXES, split_axis=0, concat_axis=0, tiled=True)  7.05 us
    pallas_call x1, Pallas kernels, turned(): pl.pallas_call(turn_kernel, out_shape=jax.ShapeDtypeStruct((TB, TB + 8, T...  5.45 us
    pallas_call x1, Pallas kernels, model_of(): pl.pallas_call(model_kernel, out_shape=jax.ShapeDtypeStruct((EXTENT, EXTE...  5.09 us
  transfers between devices with their start and end apart: 6, of which 3 were waited for; matrix products, arithmetic and copies ran while one was open for 2% of the time, Pallas kernels for 13%

profile of v5, /device:TPU:1, one launch (start us, length us, event | category | flops | bytes accessed | tf_op | source)
XLA Modules:
  0.0 106.8 jit_solution(11450676033569763895)
XLA Ops:
  0.0 5.4 %shard_map.73 = bf16[128,136,128]{2,1,0:T(8,128)(2,1)} custom-call(s32[1,128]{1,0:T(1,128)} %bitcast.14, s32[1,128]{1,0:T(1,128)} %bitcast.15, bf16[128,128,128]{2,1,0:T(8,128)(2,1)} %blocks_ref.1), custom_call_target="tpu_custom_call" | custom-call | flops 600000000 | bytes 8700000 | tf_op jit(solution)/shard_map/pallas_call | solution.py:139
  5.5 0.0 copy-start
  5.5 0.0 copy-start.2
  5.5 0.0 copy-start.3
  5.5 0.0 copy-start.4
  5.5 11.9 %all-to-all-start = ((bf16[128,136,128]{2,1,0:T(8,128)(2,1)}), bf16[128,136,128]{2,1,0:T(8,128)(2,1)}, u32[]{:S(2)}, u32[]{:S(2)}) async-start(bf16[128,136,128]{2,1,0:T(8,128)(2,1)} %shard_map.73), calls=%async_computation | async-start | bytes 8912896 | tf_op jit(solution)/shard_map/all_to_all | solution.py:230
  17.4 0.0 copy-done
  17.4 3.3 %collective-permute-start = (bf16[15,512]{1,0:T(8,128)(2,1)S(1)}, bf16[15,512]{1,0:T(8,128)(2,1)S(1)}, u32[]{:S(2)}, u32[]{:S(2)}) collective-permute-start(bf16[15,512]{1,0:T(8,128)(2,1)S(1)} %get-tuple-element.13), channel_id=1, source_target_pairs={{0,1},{1,2},{2,3},{4,5},{5,6},{6,7},{8,9},{9,10},{10,11},{12,13},{... | collective-permute-start | bytes 46088 | tf_op jit(solution)/shard_map/ppermute | solution.py:29
  20.7 1.3 %collective-permute-start.1 = (bf16[15,512]{1,0:T(8,128)(2,1)S(1)}, bf16[15,512]{1,0:T(8,128)(2,1)S(1)}, u32[]{:S(2)}, u32[]{:S(2)}) collective-permute-start(bf16[15,512]{1,0:T(8,128)(2,1)S(1)} %get-tuple-element.14), channel_id=1, source_target_pairs={{1,0},{2,1},{3,2},{5,4},{6,5},{7,6},{9,8},{10,9},{11,10},{13,12},{... | collective-permute-start | bytes 46088 | tf_op jit(solution)/shard_map/ppermute | solution.py:29
  22.1 0.0 copy-done.2
  22.1 0.0 copy-done.3
  22.1 0.1 pad_maximum_fusion.3.origin_ref
  22.2 0.0 copy-done.4
  22.2 0.1 copy.13
  22.3 0.1 reshape.29.coeffs_ref
  22.4 34.9 %collective-permute-done = bf16[15,512]{1,0:T(8,128)(2,1)S(1)} collective-permute-done((bf16[15,512]{1,0:T(8,128)(2,1)S(1)}, bf16[15,512]{1,0:T(8,128)(2,1)S(1)}, u32[]{:S(2)}, u32[]{:S(2)}) %collective-permute-start) | collective-permute-done | bytes 15392 | tf_op jit(solution)/shard_map/ppermute | solution.py:29
  57.2 6.5 %collective-permute-done.1 = bf16[15,512]{1,0:T(8,128)(2,1)S(1)} collective-permute-done((bf16[15,512]{1,0:T(8,128)(2,1)S(1)}, bf16[15,512]{1,0:T(8,128)(2,1)S(1)}, u32[]{:S(2)}, u32[]{:S(2)}) %collective-permute-start.1) | collective-permute-done | bytes 15392 | tf_op jit(solution)/shard_map/ppermute | solution.py:29
  63.7 0.1 pad_maximum_fusion.2
  63.9 7.9 %collective-permute-start.2 = (bf16[542,15]{1,0:T(8,128)(2,1)S(1)}, bf16[542,15]{1,0:T(8,128)(2,1)S(1)}, u32[]{:S(2)}, u32[]{:S(2)}) collective-permute-start(bf16[542,15]{1,0:T(8,128)(2,1)S(1)} %get-tuple-element.11), channel_id=1, source_target_pairs={{0,4},{4,8},{8,12},{12,16},{16,20},{20,24},{24,28},{28,32},{32,36}... | collective-permute-start | bytes 48788 | tf_op jit(solution)/shard_map/ppermute | solution.py:29
  71.8 1.9 %collective-permute-start.3 = (bf16[542,15]{1,0:T(8,128)(2,1)S(1)}, bf16[542,15]{1,0:T(8,128)(2,1)S(1)}, u32[]{:S(2)}, u32[]{:S(2)}) collective-permute-start(bf16[542,15]{1,0:T(8,128)(2,1)S(1)} %get-tuple-element.12), channel_id=1, source_target_pairs={{4,0},{8,4},{12,8},{16,12},{20,16},{24,20},{28,24},{32,28},{36,32}... | collective-permute-start | bytes 48788 | tf_op jit(solution)/shard_map/ppermute | solution.py:29
  73.7 0.0 all-to-all-done.arrived_ref
  73.7 9.2 %shard_map.74 = (bf16[128,16,128]{2,1,0:T(8,128)(2,1)}, f32[128,128]{1,0:T(8,128)}, f32[1,640]{1,0:T(1,128)}) custom-call(bf16[128,136,128]{2,1,0:T(8,128)(2,1)} %all-to-all-done.arrived_ref), custom_call_target="tpu_custom_call" | custom-call | flops 5000000000 | bytes 5000000 | tf_op jit(solution)/shard_map/pallas_call | solution.py:206
  83.0 0.0 copy-start.1
  83.0 8.8 %all-to-all-start.1 = ((bf16[128,16,128]{2,1,0:T(8,128)(2,1)}), bf16[128,16,128]{2,1,0:T(8,128)(2,1)S(1)}, u32[]{:S(2)}, u32[]{:S(2)}) async-start(bf16[128,16,128]{2,1,0:T(8,128)(2,1)} %get-tuple-element.8), calls=%async_computation.1 | async-start | bytes 1048576 | tf_op jit(solution)/shard_map/all_to_all | solution.py:233
  91.8 0.7 reduce
  92.5 0.0 collective-permute-done.2
  92.5 0.0 collective-permute-done.3
  92.5 0.6 add_convert_fusion.padded_ref
  93.1 0.0 copy-done.1
  93.1 0.3 convert_reduce_fusion
  93.4 5.1 %shard_map.75 = f32[512,512]{1,0:T(8,128)S(1)} custom-call(f32[27]{0:T(128)S(1)} %reshape.29.coeffs_ref, f32[2]{0:T(128)S(1)} %pad_maximum_fusion.3.origin_ref, bf16[544,640]{1,0:T(8,128)(2,1)S(1)} %add_convert_fusion.padded_ref, f32[16,256]{1,0:T(8,128)S(1)} %get-tuple-element.16.rows_ref, f32[16,256]{1,0:T(8,128)S(1)} %get-tuple-element.15.cols_ref), custom_call_target="tpu_custom_call" | custom-call | flops 3000000000 | bytes 2000000 | tf_op jit(solution)/shard_map/pallas_call | solution.py:86
  98.5 7.0 %all-to-all-done.1 = bf16[128,16,128]{2,1,0:T(8,128)(2,1)S(1)} async-done(((bf16[128,16,128]{2,1,0:T(8,128)(2,1)}), bf16[128,16,128]{2,1,0:T(8,128)(2,1)S(1)}, u32[]{:S(2)}, u32[]{:S(2)}) %all-to-all-start.1) | async-done | bytes 524320 | tf_op jit(solution)/shard_map/all_to_all | solution.py:233
  105.5 0.1 convert_multiply_fusion
  105.7 0.2 copy.12
  105.9 1.0 fusion.6
  (4 shorter events, 0.0 us)
Async XLA Ops:
  5.5 12.0 %copy-start = (bf16[512,512]{1,0:T(8,128)(2,1)S(1)}, bf16[512,512]{1,0:T(8,128)(2,1)}, u32[]{:S(2)}) copy-start(bf16[512,512]{1,0:T(8,128)(2,1)} %param.10) | copy-start | bytes 1572868
  5.5 16.6 %copy-start.2 = (bf16[9,31]{1,0:T(8,128)(2,1)S(1)}, bf16[9,31]{1,0:T(8,128)(2,1)}, u32[]{:S(2)}) copy-start(bf16[9,31]{1,0:T(8,128)(2,1)} %param.12) | copy-start | bytes 1678
  5.5 16.6 %copy-start.3 = (bf16[9,31]{1,0:T(8,128)(2,1)S(1)}, bf16[9,31]{1,0:T(8,128)(2,1)}, u32[]{:S(2)}) copy-start(bf16[9,31]{1,0:T(8,128)(2,1)} %param.11) | copy-start | bytes 1678
  5.5 16.7 %copy-start.4 = (f32[9,3]{0,1:T(4,128)S(1)}, f32[9,3]{0,1:T(4,128)}, u32[]{:S(2)}) copy-start(f32[9,3]{0,1:T(4,128)} %param.13) | copy-start | bytes 328
  5.5 68.2 %all-to-all-start = ((bf16[128,136,128]{2,1,0:T(8,128)(2,1)}), bf16[128,136,128]{2,1,0:T(8,128)(2,1)}, u32[]{:S(2)}, u32[]{:S(2)}) async-start(bf16[128,136,128]{2,1,0:T(8,128)(2,1)} %shard_map.73), calls=%async_computation | async-start | bytes 8912896 | tf_op jit(solution)/shard_map/all_to_all | solution.py:230
  17.4 39.8 %collective-permute-start = (bf16[15,512]{1,0:T(8,128)(2,1)S(1)}, bf16[15,512]{1,0:T(8,128)(2,1)S(1)}, u32[]{:S(2)}, u32[]{:S(2)}) collective-permute-start(bf16[15,512]{1,0:T(8,128)(2,1)S(1)} %get-tuple-element.13), channel_id=1, source_target_pairs={{0,1},{1,2},{2,3},{4,5},{5,6},{6,7},{8,9},{9,10},{10,11},{12,13},{... | collective-permute-start | bytes 46088 | tf_op jit(solution)/shard_map/ppermute | solution.py:29
  20.7 43.0 %collective-permute-start.1 = (bf16[15,512]{1,0:T(8,128)(2,1)S(1)}, bf16[15,512]{1,0:T(8,128)(2,1)S(1)}, u32[]{:S(2)}, u32[]{:S(2)}) collective-permute-start(bf16[15,512]{1,0:T(8,128)(2,1)S(1)} %get-tuple-element.14), channel_id=1, source_target_pairs={{1,0},{2,1},{3,2},{5,4},{6,5},{7,6},{9,8},{10,9},{11,10},{13,12},{... | collective-permute-start | bytes 46088 | tf_op jit(solution)/shard_map/ppermute | solution.py:29
  63.9 28.6 %collective-permute-start.2 = (bf16[542,15]{1,0:T(8,128)(2,1)S(1)}, bf16[542,15]{1,0:T(8,128)(2,1)S(1)}, u32[]{:S(2)}, u32[]{:S(2)}) collective-permute-start(bf16[542,15]{1,0:T(8,128)(2,1)S(1)} %get-tuple-element.11), channel_id=1, source_target_pairs={{0,4},{4,8},{8,12},{12,16},{16,20},{20,24},{24,28},{28,32},{32,36}... | collective-permute-start | bytes 48788 | tf_op jit(solution)/shard_map/ppermute | solution.py:29
  71.8 20.7 %collective-permute-start.3 = (bf16[542,15]{1,0:T(8,128)(2,1)S(1)}, bf16[542,15]{1,0:T(8,128)(2,1)S(1)}, u32[]{:S(2)}, u32[]{:S(2)}) collective-permute-start(bf16[542,15]{1,0:T(8,128)(2,1)S(1)} %get-tuple-element.12), channel_id=1, source_target_pairs={{4,0},{8,4},{12,8},{16,12},{20,16},{24,20},{28,24},{32,28},{36,32}... | collective-permute-start | bytes 48788 | tf_op jit(solution)/shard_map/ppermute | solution.py:29
  83.0 10.1 %copy-start.1 = (f32[128,128]{1,0:T(8,128)S(1)}, f32[128,128]{1,0:T(8,128)}, u32[]{:S(2)}) copy-start(f32[128,128]{1,0:T(8,128)} %get-tuple-element.9) | copy-start | bytes 196612
  83.0 22.6 %all-to-all-start.1 = ((bf16[128,16,128]{2,1,0:T(8,128)(2,1)}), bf16[128,16,128]{2,1,0:T(8,128)(2,1)S(1)}, u32[]{:S(2)}, u32[]{:S(2)}) async-start(bf16[128,16,128]{2,1,0:T(8,128)(2,1)} %get-tuple-element.8), calls=%async_computation.1 | async-start | bytes 1048576 | tf_op jit(solution)/shard_map/all_to_all | solution.py:233
